TPU v7x, 256 devices: a whole 4x4x8 slice. The times are simulated.
256 devices in a mesh: dp: 32 (over y_lo, z, core), cores: 8 (over y_hi, x).
Axes of the slice: x: 4, y: 4 (y_hi: 2, y_lo: 2; y = y_hi * 2 + y_lo), z: 8, core: 2. Of those that a mesh axis runs over, the one named last changes fastest.
Arguments:
- tokens: bfloat16 [8192, 6144], P('dp', 'cores'), may hold values from -6 to 6
- router_weight: bfloat16 [256, 6144], P(None, 'cores'), may hold values from -0.078125 to 0.078125
- expert_factor: bfloat16 [256, 64], P(None, 'cores'), may hold values from -0.375 to 0.375
- input_factor: bfloat16 [512, 6144], P(None, 'cores'), may hold values from -0.078125 to 0.078125
- core_tensor: bfloat16 [512, 64, 512], P('dp', 'cores'), may hold values from -0.03125 to 0.03125
- output_factor: bfloat16 [512, 6144], P(None, 'cores'), may hold values from -0.25 to 0.25
- out_grad: bfloat16 [8192, 6144], P('dp', 'cores'), may hold values from -6 to 6
Outputs:
- mixed: bfloat16 [8192, 6144], P('dp', 'cores')
- token_grad: bfloat16 [8192, 6144], P('dp', 'cores')
- core_grad: float32 [512, 64, 512], P('dp', 'cores')
- input_grad: float32 [512, 6144], P('dp', 'cores')
- router_grad: float32 [256, 6144], P('dp', 'cores')
- output_grad: float32 [512, 6144], P('dp', 'cores')
- expert_grad: float32 [256, 64], P('dp', 'cores')
All inputs are finite; a program needn't handle non-finite values.
Results may differ from a plain program's by a relative error of at most 0.0066.
Values may be sent and summed in bfloat16 or wider, within the bound.
A program may use at most 64 MiB of HBM per device.

v0:
```python
import jax
import jax.numpy as jnp
from jax import lax
from jax.sharding import PartitionSpec as P


def shards(
    tokens, router_weight, expert_factor, input_factor, core_tensor, output_factor, out_grad
):
    highest = lax.Precision.HIGHEST
    row_count = tokens.shape[0]
    local_experts = core_tensor.shape[1]
    out_rank = core_tensor.shape[2]
    inv_rows = 1.0 / row_count
    logit_part = jnp.einsum("td,gd->tg", tokens, router_weight, preferred_element_type=jnp.float32)
    proj_part = jnp.einsum("td,id->ti", tokens, input_factor, preferred_element_type=jnp.float32)
    back_part = jnp.einsum("td,od->to", out_grad, output_factor, preferred_element_type=jnp.float32)
    logits, proj_sum, back_sum = lax.psum((logit_part, proj_part, back_part), "cores")
    gate_values = jax.nn.sigmoid(logits)
    gate_low = gate_values.astype(jnp.bfloat16)
    mixing = jnp.dot(gate_low, expert_factor, preferred_element_type=jnp.float32)
    projected = proj_sum.astype(jnp.bfloat16)
    latent_grad = back_sum.astype(jnp.bfloat16)
    whole_core = lax.all_gather(core_tensor, "dp", axis=0, tiled=True)
    expanded = jnp.dot(
        projected,
        whole_core.reshape(whole_core.shape[0], local_experts * out_rank),
        preferred_element_type=jnp.float32,
    )
    latent_part = jnp.einsum(
        "te,teo->to",
        mixing,
        expanded.reshape(row_count, local_experts, out_rank),
        precision=highest,
    )
    latent = lax.psum(latent_part, "cores").astype(jnp.bfloat16)
    mixed = jnp.dot(latent, output_factor, preferred_element_type=jnp.float32).astype(jnp.bfloat16)
    spread = jnp.einsum("to,ieo->tei", latent_grad, whole_core, preferred_element_type=jnp.float32)
    mixing_grad = jnp.einsum("ti,tei->te", projected.astype(jnp.float32), spread, precision=highest)
    projgrad_part = jnp.einsum("te,tei->ti", mixing, spread, precision=highest)
    mixing_low = mixing_grad.astype(jnp.bfloat16)
    gate_part = jnp.einsum(
        "te,ge->tg", mixing_low, expert_factor, preferred_element_type=jnp.float32
    )
    projgrad_sum, gate_grad = lax.psum((projgrad_part, gate_part), "cores")
    outer = (mixing[:, :, None] * latent_grad[:, None, :].astype(jnp.float32)).astype(jnp.bfloat16)
    outer_flat = outer.reshape(row_count, local_experts * out_rank)
    core_term = (
        jnp.einsum("ti,tk->ik", projected, outer_flat, preferred_element_type=jnp.float32)
        * inv_rows
    )
    core_grad = lax.psum_scatter(
        core_term.reshape(core_term.shape[0], local_experts, out_rank),
        "dp",
        scatter_dimension=0,
        tiled=True,
    )
    logit_grad = (gate_grad * gate_values * (1.0 - gate_values)).astype(jnp.bfloat16)
    projected_grad = projgrad_sum.astype(jnp.bfloat16)
    token_sum = jnp.dot(projected_grad, input_factor, preferred_element_type=jnp.float32) + jnp.dot(
        logit_grad, router_weight, preferred_element_type=jnp.float32
    )
    token_grad = token_sum.astype(jnp.bfloat16)
    input_term = (
        jnp.einsum("ti,td->id", projected_grad, tokens, preferred_element_type=jnp.float32)
        * inv_rows
    )
    router_term = (
        jnp.einsum("tg,td->gd", logit_grad, tokens, preferred_element_type=jnp.float32) * inv_rows
    )
    output_term = (
        jnp.einsum("to,td->od", latent, out_grad, preferred_element_type=jnp.float32) * inv_rows
    )
    expert_term = (
        jnp.einsum("tg,te->ge", gate_low, mixing_low, preferred_element_type=jnp.float32) * inv_rows
    )
    input_grad, router_grad, output_grad, expert_grad = (
        lax.psum_scatter(input_term, "dp", scatter_dimension=0, tiled=True),
        lax.psum_scatter(router_term, "dp", scatter_dimension=0, tiled=True),
        lax.psum_scatter(output_term, "dp", scatter_dimension=0, tiled=True),
        lax.psum_scatter(expert_term, "dp", scatter_dimension=0, tiled=True),
    )
    return (mixed, token_grad, core_grad, input_grad, router_grad, output_grad, expert_grad)


def solution(mesh):
    return jax.shard_map(
        shards,
        mesh=mesh,
        in_specs=(
            P("dp", "cores"),
            P(None, "cores"),
            P(None, "cores"),
            P(None, "cores"),
            P("dp", "cores", None),
            P(None, "cores"),
            P("dp", "cores"),
        ),
        out_specs=(
            P("dp", "cores"),
            P("dp", "cores"),
            P("dp", "cores", None),
            P("dp", "cores"),
            P("dp", "cores"),
            P("dp", "cores"),
            P("dp", "cores"),
        ),
        check_vma=False,
    )
```

profile of v0, /device:TPU:2, one launch (start us, length us, event | category | flops | bytes accessed | tf_op | source)
XLA Modules:
  0.0 681.8 jit_solution(5500845968447808366)
XLA Ops:
  7.2 1.7 copy.19
  9.0 1.7 fusion.27
  10.6 1.4 fusion.28
  12.0 2.1 fusion.26
  14.2 77.2 %all-reduce.9 = (bf16[256,512]{1,0:T(8,128)(2,1)S(1)}, bf16[256,512]{1,0:T(8,128)(2,1)S(1)}) all-reduce(f32[256,512]{1,0:T(8,128)S(1)} %fusion.27, f32[256,512]{1,0:T(8,128)S(1)} %fusion.28), channel_id=1, replica_groups=mesh['dp'=32,'cores'=8] {'cores'}, use_global_device_ids=true, to_apply=%region_1.0 | all-reduce | flops 262144 | bytes 1572864 | tf_op jit(solution)/shard_map/psum | solution.py:18
  91.4 3.5 fusion.10
  94.9 1.9 copy-done.1
  96.8 5.6 fusion.4
  102.5 0.9 fusion.23
  103.4 6.5 copy.20
  109.9 5.5 fusion
  115.4 76.5 %all-reduce.8.cloned.1.call-done = (f32[256,256]{1,0:T(8,128)}, f32[256,256]{1,0:T(8,128)}) async-done(((f32[256,256]{1,0:T(8,128)}, f32[256,256]{1,0:T(8,128)}), (f32[256,256]{1,0:T(8,128)}, f32[256,256]{1,0:T(8,128)})) %all-reduce.8.cloned.1.call-update) | async-done | bytes 524304 | tf_op jit(solution)/shard_map/psum | solution.py:18
  191.8 1.1 multiply_convert_fusion.1
  193.0 1.2 convolution_multiply_fusion.3
  194.4 1.1 fusion.20
  195.7 8.4 %fusion.2 = f32[256,1,512]{2,1,0:T(1,128)S(1)} fusion(f32[256,8,1]{1,2,0:T(1,128)S(1)} %copy.22, f32[256,8,512]{2,0,1:T(8,128)} %fusion), kind=kOutput, calls=%fused_computation.3 | convolution fusion | flops 12582912 | bytes 4726784 | tf_op jit(solution)/shard_map/te,teo->to/dot_general | solution.py:30
  204.2 5.4 fusion.6
  209.6 79.3 %all-reduce.10 = (bf16[256,512]{1,0:T(8,128)(2,1)}, bf16[256,512]{1,0:T(8,128)(2,1)S(1)}) all-reduce(f32[256,512]{1,0:T(8,128)S(1)} %bitcast.59, f32[256,512]{1,0:T(8,128)S(1)} %bitcast.60), channel_id=1, replica_groups=mesh['dp'=32,'cores'=8] {'cores'}, use_global_device_ids=true, to_apply=%region_2.0 | all-reduce | flops 262144 | bytes 1572864 | tf_op jit(solution)/shard_map/psum | solution.py:36
  289.0 1.6 convolution_multiply_fusion.2
  290.7 2.5 convolution_multiply_fusion.1
  294.0 0.9 copy.29
  294.9 1.3 convolution_multiply_fusion
  296.2 11.3 %copy.30 = f32[64,8,8,512]{3,2,1,0:T(8,128)} copy(f32[64,8,8,512]{3,1,2,0:T(8,128)S(1)} %bitcast.55) | data formatting | bytes 16777216
  307.6 0.6 copy-done.12
  308.2 0.6 dynamic-slice
  309.8 104.6 %all-reduce = f32[256,8]{1,0:T(8,128)S(1)} all-reduce(f32[256,8]{1,0:T(8,128)S(1)} %convolution_multiply_fusion.4), channel_id=6, replica_groups=mesh['dp'=32,'cores'=8] {'dp'}, use_global_device_ids=true, to_apply=%region_10.0.clone | all-reduce | flops 2048 | bytes 16384
  414.3 0.6 constant_dynamic-slice_fusion
  414.9 1.1 convolution_convert_fusion
  416.4 1.0 fusion.8
  417.4 12.9 %reduce-scatter.7.cloned.1.call-done = f32[16,768]{1,0:T(8,128)} async-done(((f32[512,768]{1,0:T(8,128)}), f32[16,768]{1,0:T(8,128)}) %reduce-scatter.7.cloned.1.call-update) | async-done | bytes 49168 | tf_op jit(solution)/shard_map/reduce_scatter | solution.py:78
  430.3 116.5 %reduce-scatter.11.cloned.1.call-done = f32[16,768]{1,0:T(8,128)} async-done(((f32[512,768]{1,0:T(8,128)}), f32[16,768]{1,0:T(8,128)}) %reduce-scatter.11.cloned.1.call-update) | async-done | bytes 49168 | tf_op jit(solution)/shard_map/reduce_scatter | solution.py:80
  546.9 128.1 %reduce-scatter.5.cloned.1.call-done = f32[16,8,512]{2,1,0:T(8,128)} async-done(((f32[512,8,512]{2,1,0:T(8,128)}), f32[16,8,512]{2,1,0:T(8,128)}) %reduce-scatter.5.cloned.1.call-update) | async-done | bytes 262160 | tf_op jit(solution)/shard_map/reduce_scatter | solution.py:52
  (46 shorter events, 2.2 us)
Async XLA Ops:
  7.2 3.5 copy-start
  7.2 84.2 %all-gather.2.cloned.1.call-start = ((), (), s32[]{:S(2)}) async-start(), calls=%async_computation.4 | async-start | bytes 4325376 | tf_op jit(solution)/shard_map/all_gather | solution.py:24
  8.9 182.9 %all-reduce.8.cloned.1.call-start = ((), (), s32[]{:S(2)}) async-start(), calls=%async_computation.9 | async-start | bytes 1048576 | tf_op jit(solution)/shard_map/psum | solution.py:18
  94.8 2.0 copy-start.1
  94.9 7.6 %copy-start.11 = (bf16[256,8]{0,1:T(8,128)(2,1)S(1)}, bf16[256,8]{0,1:T(8,128)(2,1)}, u32[]{:S(2)}) copy-start(bf16[256,8]{0,1:T(8,128)(2,1)} %param.9) | copy-start | bytes 12292
  102.4 7.4 %copy-start.8 = (f32[256,1,8]{2,1,0:T(1,128)}, f32[256,1,8]{2,1,0:T(1,128)S(1)}, u32[]{:S(2)}) copy-start(f32[256,1,8]{2,1,0:T(1,128)S(1)} %fusion.4) | copy-start | bytes 24580
  103.3 314.1 %reduce-scatter.9.cloned.1.call-start = ((), (), s32[]{:S(2)}) async-start(), calls=%async_computation.7 | async-start | bytes 811008 | tf_op jit(solution)/shard_map/reduce_scatter | solution.py:79
  109.9 83.1 %copy-start.3 = (bf16[256,768]{1,0:T(8,128)(2,1)S(1)}, bf16[256,768]{1,0:T(8,128)(2,1)}, u32[]{:S(2)}) copy-start(bf16[256,768]{1,0:T(8,128)(2,1)} %param.7) | copy-start | bytes 1179652
  194.2 236.1 %reduce-scatter.7.cloned.1.call-start = ((), (), s32[]{:S(2)}) async-start(), calls=%async_computation.6 | async-start | bytes 1622016 | tf_op jit(solution)/shard_map/reduce_scatter | solution.py:78
  195.7 8.4 %copy-start.2 = (f32[256,512,8]{1,0,2:T(8,128)S(1)}, f32[256,512,8]{1,0,2:T(8,128)}, u32[]{:S(2)}) copy-start(f32[256,512,8]{1,0,2:T(8,128)} %copy-done.1) | copy-start | bytes 12582916
  204.1 86.5 %copy-start.6 = (bf16[256,768]{1,0:T(8,128)(2,1)S(1)}, bf16[256,768]{1,0:T(8,128)(2,1)}, u32[]{:S(2)}) copy-start(bf16[256,768]{1,0:T(8,128)(2,1)} %param.13) | copy-start | bytes 1179652
  290.6 256.3 %reduce-scatter.11.cloned.1.call-start = ((), (), s32[]{:S(2)}) async-start(), calls=%async_computation.8 | async-start | bytes 1622016 | tf_op jit(solution)/shard_map/reduce_scatter | solution.py:80
  293.2 381.8 %reduce-scatter.5.cloned.1.call-start = ((), (), s32[]{:S(2)}) async-start(), calls=%async_computation.5 | async-start | bytes 8650752 | tf_op jit(solution)/shard_map/reduce_scatter | solution.py:52
  307.5 0.7 copy-start.12
  307.5 1.9 copy-start.9
  307.6 1.9 copy-start.10
  307.6 107.4 %copy-start.7 = (bf16[256,512]{1,0:T(8,128)(2,1)S(1)}, bf16[256,512]{1,0:T(8,128)(2,1)}, u32[]{:S(2)}) copy-start(bf16[256,512]{1,0:T(8,128)(2,1)} %get-tuple-element.7) | copy-start | bytes 786436
  307.6 108.5 %copy-start.4 = (bf16[512,768]{1,0:T(8,128)(2,1)S(1)}, bf16[512,768]{1,0:T(8,128)(2,1)}, u32[]{:S(2)}) copy-start(bf16[512,768]{1,0:T(8,128)(2,1)} %param.10) | copy-start | bytes 2359300
  307.6 108.8 %copy-start.5 = (bf16[256,768]{1,0:T(8,128)(2,1)S(1)}, bf16[256,768]{1,0:T(8,128)(2,1)}, u32[]{:S(2)}) copy-start(bf16[256,768]{1,0:T(8,128)(2,1)} %param.8) | copy-start | bytes 1179652
Sparse Core Ops, SparseCore 0:
  10.5 69.7 all-gather.1
  103.5 88.3 all-reduce.7
  195.1 117.7 reduce-scatter.8
  315.8 114.4 reduce-scatter.6
  433.4 113.3 reduce-scatter.10
  549.8 125.1 reduce-scatter.4
where the time goes:
time: 682 us
  waiting for transfers between devices  334 us (49%)
  blocking collectives  261 us (38%)
  matrix products  44.9 us (7%)
  local copies, waits for them, and re-layouts  24.5 us (4%)
  between operations  15 us (2%)
    reduce_scatter x1, waiting for transfers between devices, shards(): lax.psum_scatter(core_term.reshape(core_term.shape[0], local_experts, out...  128 us
    reduce_scatter x1, waiting for transfers between devices, shards(): lax.psum_scatter(output_term, 'dp', scatter_dimension=0, tiled=True)  117 us
    unnamed x1, blocking collectives  105 us
    psum x1, blocking collectives, shards(): latent = lax.psum(latent_part, 'cores').astype(jnp.bfloat16)  79.3 us
    psum x1, blocking collectives, shards(): lax.psum((logit_part, proj_part, back_part), 'cores')  77.2 us
    psum x1, waiting for transfers between devices, shards(): lax.psum((logit_part, proj_part, back_part), 'cores')  76.5 us
    unnamed x31, local copies, waits for them, and re-layouts  17.7 us
  transfers between devices with their start and end apart: 6, of which 4 were waited for; matrix products, arithmetic and copies ran while one was open for 8% of the time, Pallas kernels for 0%

commit v1 on v0

v1 whole, which is shorter than its diff:
```python
import functools

import jax
import jax.numpy as jnp
from jax import lax
from jax.experimental import pallas as pl
from jax.experimental.pallas import tpu as pltpu
from jax.sharding import PartitionSpec as P

MESH = pl.DeviceIdType.MESH
F32 = jnp.float32
BF16 = jnp.bfloat16


def dot_nn(a, b):
    return lax.dot_general(a, b, (((1,), (0,)), ((), ())), preferred_element_type=F32)


def dot_nt(a, b):
    return lax.dot_general(a, b, (((1,), (1,)), ((), ())), preferred_element_type=F32)


def dot_tn(a, b):
    return lax.dot_general(a, b, (((0,), (0,)), ((), ())), preferred_element_type=F32)


def ring_hops(n_z):
    up = n_z // 2
    down = n_z - 1 - up
    return ((up, down), (down, up))


class Ids:
    def __init__(self, n_z, n_cores, n_e):
        self.count = 0
        steps = n_z // 2
        self.gather_y = self.take(1)
        self.gather_z = self.take(4 * steps)
        self.gather_sib = self.take(2 * n_z)
        self.factor = self.take(n_cores - 1)
        self.sum_in = self.take(n_cores - 1)
        self.share_in = self.take(n_cores - 1)
        self.sum_mid = self.take(n_cores - 1)
        self.share_mid = self.take(n_cores - 1)
        self.core_sib = self.take(n_e)
        self.core_z = self.take(4 * steps)
        self.core_y = self.take(1)
        self.fac_sib = self.take(1)
        self.fac_z = self.take(4 * steps)
        self.fac_y = self.take(1)

    def take(self, n):
        first = self.count
        self.count += n
        return first


def kernel(
    n_z, n_cores,
    tok_hbm, rw_hbm, ef_hbm, inf_hbm, core_hbm, outf_hbm, og_hbm,
    mixed_ref, tgrad_ref, cgrad_ref, igrad_ref, rgrad_ref, ograd_ref, egrad_ref,
    tok, rw, ef, inf, outf, og,
    whole, ef_all, part_in, got_in, held_in, gates, part_mid, got_mid, held_mid,
    mix_b, outer, lat_acc, pg_acc, mg_acc,
    core_b, core_s, core_r, core_yr,
    fac_b, fac_s, fac_r, fac_yr,
    in_sem, ss, rs,
):
    rows, width = tok.shape
    n_g = rw.shape[0]
    n_i = inf.shape[0]
    n_o = outf.shape[0]
    n_e = ef.shape[0]
    block = rows // n_cores
    i_rows = whole.shape[4]
    n_dp = 4 * n_z
    inv_rows = 1.0 / rows
    ids = Ids(n_z, n_cores, n_e)
    steps = n_z // 2
    hops = ring_hops(n_z)

    dp = lax.axis_index("dp")
    c = lax.axis_index("cores")
    core = lax.rem(dp, 2)
    z = lax.rem(dp // 2, n_z)
    y = dp // (2 * n_z)

    def at(yy, zz, kk):
        return ((yy * n_z + zz) * 2 + kk, c)

    def zmod(offset):
        return lax.rem(z + offset + 2 * n_z, n_z)

    sib = at(y, z, 1 - core)
    ynb = at(1 - y, z, core)
    znb = (at(y, zmod(1), core), at(y, zmod(-1), core))
    n_x = n_cores // 2
    y_hi = c // n_x
    x = lax.rem(c, n_x)
    peers = []
    for dy in range(2):
        for dx in range(n_x):
            if dy or dx:
                other = lax.rem(y_hi + dy, 2) * n_x + lax.rem(x + dx, n_x)
                peers.append((dp, other))

    sent = []

    def send(i, src, dst, dev):
        d = pltpu.make_async_remote_copy(
            src, dst, ss.at[i], rs.at[i], device_id=dev, device_id_type=MESH
        )
        d.start()
        sent.append(d)

    def arrive(i, ref):
        pltpu.make_async_remote_copy(
            ref, ref, ss.at[i], rs.at[i], device_id=sib, device_id_type=MESH
        ).wait_recv()

    loads = [
        pltpu.make_async_copy(src, dst, in_sem.at[n])
        for n, (src, dst) in enumerate(
            (
                (core_hbm, whole.at[y, z, core]),
                (tok_hbm, tok),
                (inf_hbm, inf),
                (og_hbm, og),
                (outf_hbm, outf),
                (rw_hbm, rw),
                (ef_hbm, ef),
            )
        )
    ]
    for load in loads:
        load.start()

    barrier = pltpu.get_barrier_semaphore()
    greet = [sib, ynb, znb[0], znb[1]] + peers
    for dev in greet:
        pl.semaphore_signal(barrier, inc=1, device_id=dev, device_id_type=MESH)
    pl.semaphore_wait(barrier, len(greet))

    lane_y = (y, 1 - y)

    def ag_id(lane, way, s):
        return ids.gather_z + (lane * 2 + way) * steps + s - 1

    def ag_ref(lane, zz):
        return whole.at[lane_y[lane], zz, core]

    def ag_sib(lane, offset):
        ref = ag_ref(lane, zmod(offset))
        send(ids.gather_sib + lane * n_z + offset % n_z, ref, ref, sib)

    def ag_open(lane):
        ref = ag_ref(lane, z)
        for way in range(2):
            if hops[lane][way] >= 1:
                send(ag_id(lane, way, 1), ref, ref, znb[way])
        ag_sib(lane, 0)

    def ag_step(s, lane):
        for way in range(2):
            if s <= hops[lane][way]:
                offset = -s if way == 0 else s
                ref = ag_ref(lane, zmod(offset))
                arrive(ag_id(lane, way, s), ref)
                if s + 1 <= hops[lane][way]:
                    send(ag_id(lane, way, s + 1), ref, ref, znb[way])
                ag_sib(lane, offset)

    def ag_close():
        for lane in range(2):
            for offset in range(n_z):
                ref = whole.at[lane_y[lane], zmod(offset), 1 - core]
                arrive(ids.gather_sib + lane * n_z + offset, ref)

    loads[0].wait()
    send(ids.gather_y, ag_ref(0, z), ag_ref(0, z), ynb)
    ag_open(0)

    loads[6].wait()
    ef_all[c] = ef[...].astype(F32)
    for k, dev in enumerate(peers):
        send(ids.factor + k, ef_all.at[c], ef_all.at[c], dev)
    loads[1].wait()
    loads[2].wait()
    part_in[:, :, n_g : n_g + n_i] = (
        dot_nt(tok[...], inf[...]).reshape(n_cores, block, n_i)
    )
    loads[3].wait()
    loads[4].wait()
    part_in[:, :, n_g + n_i :] = (
        dot_nt(og[...], outf[...]).reshape(n_cores, block, n_o)
    )
    loads[5].wait()
    part_in[:, :, :n_g] = dot_nt(tok[...], rw[...]).reshape(n_cores, block, n_g)
    for k, dev in enumerate(peers):
        send(ids.sum_in + k, part_in.at[dev[1]], got_in.at[k], dev)

    arrive(ids.gather_y, ag_ref(1, z))
    ag_open(1)
    ag_step(1, 0)

    for k in range(n_cores - 1):
        arrive(ids.sum_in + k, got_in.at[k])
    total = part_in[c]
    for k in range(n_cores - 1):
        total = total + got_in[k]
    gate = jax.nn.sigmoid(total[:, :n_g])
    gates[...] = gate
    held_in[c, :, :n_g] = gate.astype(BF16)
    held_in[c, :, n_g:] = total[:, n_g:].astype(BF16)
    for k, dev in enumerate(peers):
        send(ids.share_in + k, held_in.at[c], held_in.at[c], dev)

    ag_step(1, 1)
    ag_step(2, 0)

    for k in range(n_cores - 1):
        ref = held_in.at[peers_from(y_hi, x, n_x)[k]]
        arrive(ids.share_in + k, ref)

    gate_low = held_in[:, :, :n_g].reshape(rows, n_g)
    proj = held_in[:, :, n_g : n_g + n_i].reshape(rows, n_i)
    lgrad = held_in[:, :, n_g + n_i :].reshape(rows, n_o)
    mixing = dot_nt(gate_low, ef[...])
    for e in range(n_e):
        mix_b[e] = jnp.broadcast_to(mixing[:, e : e + 1], (rows, 128))

    def wide(v, n):
        return jnp.concatenate([v] * (n // 128), axis=1)

    proj_t = proj.T
    lgrad_wide = lgrad.astype(F32)

    def core_terms(e, _):
        o = (wide(mix_b[e], n_o) * lgrad_wide).astype(BF16)
        outer[e] = o
        term = dot_nn(proj_t, o) * inv_rows
        core_b[:, :, :, e] = term.astype(BF16).reshape(2, n_z, 2, i_rows, n_o)
        pltpu.make_async_remote_copy(
            core_b.at[:, :, 1 - core, e],
            core_s.at[:, :, e],
            ss.at[ids.core_sib + e],
            rs.at[ids.core_sib + e],
            device_id=sib,
            device_id_type=MESH,
        ).start()
        return 0

    lax.fori_loop(0, n_e, core_terms, 0)

    ag_step(2, 1)
    for s in range(3, steps + 1):
        ag_step(s, 0)
        ag_step(s, 1)

    def rs_step(s, src, sib_got, got, first):
        for lane in range(2):
            for way in range(2):
                k = hops[lane][way]
                if s <= k:
                    far = k - s + 1
                    d = zmod(far if way == 0 else -far)
                    val = src[lane_y[lane], d, core].astype(F32) + sib_got[
                        lane_y[lane], d
                    ].astype(F32)
                    if s > 1:
                        arrive(first + (lane * 2 + way) * steps + s - 2, got.at[lane, way, s - 2])
                        val = val + got[lane, way, s - 2].astype(F32)
                    src[lane_y[lane], d, core] = val.astype(BF16)
                    send(
                        first + (lane * 2 + way) * steps + s - 1,
                        src.at[lane_y[lane], d, core],
                        got.at[lane, way, s - 1],
                        znb[way],
                    )

    def rs_lane(lane, src, sib_got, got, first):
        val = src[lane_y[lane], z, core].astype(F32) + sib_got[lane_y[lane], z].astype(F32)
        for way in range(2):
            k = hops[lane][way]
            if k:
                arrive(first + (lane * 2 + way) * steps + k - 1, got.at[lane, way, k - 1])
                val = val + got[lane, way, k - 1].astype(F32)
        return val

    def rs_turn(src, sib_got, got, yr, first, y_id):
        val = rs_lane(1, src, sib_got, got, first)
        src[1 - y, z, core] = val.astype(BF16)
        send(y_id, src.at[1 - y, z, core], yr, ynb)

    def rs_end(src, sib_got, got, yr, first, y_id):
        val = rs_lane(0, src, sib_got, got, first)
        arrive(y_id, yr)
        return val + yr[...].astype(F32)

    core_args = (core_b, core_s, core_r)
    fac_args = (fac_b, fac_s, fac_r)

    for e in range(n_e):
        arrive(ids.core_sib + e, core_s.at[:, :, e])
    rs_step(1, *core_args, ids.core_z)

    ag_close()

    lat_acc[...] = jnp.zeros_like(lat_acc)
    pg_acc[...] = jnp.zeros_like(pg_acc)
    mg_acc[...] = jnp.zeros_like(mg_acc)
    lane_no = lax.broadcasted_iota(jnp.int32, (rows, 128), 1)

    def middle(e, _):
        core_e = whole[:, :, :, e].reshape(n_i, n_o)
        expanded = dot_nn(proj, core_e)
        lat_acc[...] += wide(mix_b[e], n_o) * expanded
        col = jnp.sum(lgrad_wide * expanded, axis=1, keepdims=True)
        mg_acc[...] += jnp.where(lane_no == c * n_e + e, col, 0.0)
        pg_acc[...] += dot_nt(outer[e], core_e)
        return 0

    lax.fori_loop(0, n_e, middle, 0)

    part_mid[:, :, :n_o] = lat_acc[...].astype(BF16).reshape(n_cores, block, n_o)
    part_mid[:, :, n_o : n_o + n_i] = pg_acc[...].astype(BF16).reshape(n_cores, block, n_i)
    mix_low = mg_acc[...].astype(BF16)
    part_mid[:, :, n_o + n_i :] = mix_low.reshape(n_cores, block, 128)
    for k, dev in enumerate(peers):
        send(ids.sum_mid + k, part_mid.at[dev[1]], got_mid.at[k], dev)

    expert_full = lax.dot_general(
        gate_low, mix_low, (((0,), (0,)), ((), ())), preferred_element_type=F32
    ) * inv_rows
    pick = (
        lax.broadcasted_iota(jnp.int32, (128, 128), 0)
        == lax.broadcasted_iota(jnp.int32, (128, 128), 1) + c * n_e
    ).astype(BF16)
    expert_term = dot_nn(expert_full.astype(BF16), pick)

    rs_step(2, *core_args, ids.core_z)

    for k in range(n_cores - 1):
        arrive(ids.factor + k, ef_all.at[peers_from(y_hi, x, n_x)[k]])
    for k in range(n_cores - 1):
        arrive(ids.sum_mid + k, got_mid.at[k])
    total = part_mid[c].astype(F32)
    for k in range(n_cores - 1):
        total = total + got_mid[k].astype(F32)
    mix_block = total[:, n_o + n_i : n_o + n_i + n_cores * n_e].astype(BF16)
    gate_grad = dot_nn(mix_block, ef_all[...].reshape(n_cores * n_e, n_g).astype(BF16))
    gate = gates[...]
    held_mid[c, :, : n_o + n_i] = total[:, : n_o + n_i].astype(BF16)
    held_mid[c, :, n_o + n_i :] = (gate_grad * gate * (1.0 - gate)).astype(BF16)
    for k, dev in enumerate(peers):
        send(ids.share_mid + k, held_mid.at[c], held_mid.at[c], dev)

    rs_step(3, *core_args, ids.core_z)

    for k in range(n_cores - 1):
        arrive(ids.share_mid + k, held_mid.at[peers_from(y_hi, x, n_x)[k]])
    latent = held_mid[:, :, :n_o].reshape(rows, n_o)
    pgrad = held_mid[:, :, n_o : n_o + n_i].reshape(rows, n_i)
    logit_grad = held_mid[:, :, n_o + n_i :].reshape(rows, n_g)
    blk = (2, n_z, 2)
    fac_b[:, :, :, :i_rows] = (
        (dot_tn(pgrad, tok[...]) * inv_rows).astype(BF16).reshape(*blk, i_rows, width)
    )
    fac_b[:, :, :, i_rows : 2 * i_rows] = (
        (dot_tn(latent, og[...]) * inv_rows).astype(BF16).reshape(*blk, i_rows, width)
    )
    g_rows = n_g // n_dp
    router_term = (dot_tn(logit_grad, tok[...]) * inv_rows).reshape(*blk, g_rows, width)
    expert_wide = jnp.concatenate(
        [expert_term, jnp.zeros((n_g, width - 128), F32)], axis=1
    ) if width > 128 else expert_term
    fac_b[:, :, :, 2 * i_rows :] = jnp.concatenate(
        [router_term, expert_wide.reshape(*blk, g_rows, width)], axis=3
    ).astype(BF16)
    send(ids.fac_sib, fac_b.at[:, :, 1 - core], fac_s, sib)

    rs_step(4, *core_args, ids.core_z)
    for s in range(5, steps + 1):
        rs_step(s, *core_args, ids.core_z)

    arrive(ids.fac_sib, fac_s)
    rs_step(1, *fac_args, ids.fac_z)
    rs_turn(*core_args, core_yr, ids.core_z, ids.core_y)
    mixed_ref[...] = dot_nn(latent, outf[...]).astype(BF16)
    rs_step(2, *fac_args, ids.fac_z)
    tgrad_ref[...] = (dot_nn(pgrad, inf[...]) + dot_nn(logit_grad, rw[...])).astype(BF16)
    for s in range(3, steps + 1):
        rs_step(s, *fac_args, ids.fac_z)
    cgrad_ref[...] = rs_end(*core_args, core_yr, ids.core_z, ids.core_y)
    rs_turn(*fac_args, fac_yr, ids.fac_z, ids.fac_y)
    val = rs_end(*fac_args, fac_yr, ids.fac_z, ids.fac_y)
    igrad_ref[...] = val[:i_rows]
    ograd_ref[...] = val[i_rows : 2 * i_rows]
    rgrad_ref[...] = val[2 * i_rows : 2 * i_rows + g_rows]
    egrad_ref[...] = val[2 * i_rows + g_rows :, :n_e]

    for d in sent:
        d.wait_send()

    def drain(e, _):
        pltpu.make_async_remote_copy(
            core_b.at[:, :, 1 - core, e],
            core_s.at[:, :, e],
            ss.at[ids.core_sib + e],
            rs.at[ids.core_sib + e],
            device_id=sib,
            device_id_type=MESH,
        ).wait_send()
        return 0

    lax.fori_loop(0, n_e, drain, 0)


def peers_from(y_hi, x, n_x):
    out = []
    for dy in range(2):
        for dx in range(n_x):
            if dy or dx:
                out.append(lax.rem(y_hi + dy, 2) * n_x + lax.rem(x + n_x - dx, n_x))
    return out


def shards(n_dp, n_cores, tokens, router_weight, expert_factor, input_factor, core_tensor,
           output_factor, out_grad):
    n_z = n_dp // 4
    steps = n_z // 2
    rows, width = tokens.shape
    n_g = router_weight.shape[0]
    n_i = input_factor.shape[0]
    n_o = output_factor.shape[0]
    i_rows, n_e, _ = core_tensor.shape
    g_rows = n_g // n_dp
    block = rows // n_cores
    core_in = jnp.transpose(core_tensor, (1, 0, 2))
    cblk = (n_e, i_rows, n_o)
    fblk = (2 * i_rows + 2 * g_rows, width)
    in_cols = n_g + n_i + n_o
    mid_cols = n_o + n_i + 128
    ids = Ids(n_z, n_cores, n_e)
    vmem = pltpu.VMEM
    scratch = [
        vmem((rows, width), BF16),
        vmem((n_g, width), BF16),
        vmem((n_e, n_g), BF16),
        vmem((n_i, width), BF16),
        vmem((n_o, width), BF16),
        vmem((rows, width), BF16),
        vmem((2, n_z, 2) + cblk, BF16),
        vmem((n_cores, n_e, n_g), F32),
        vmem((n_cores, block, in_cols), F32),
        vmem((n_cores - 1, block, in_cols), F32),
        vmem((n_cores, block, in_cols), BF16),
        vmem((block, n_g), F32),
        vmem((n_cores, block, mid_cols), BF16),
        vmem((n_cores - 1, block, mid_cols), BF16),
        vmem((n_cores, block, in_cols), BF16),
        vmem((n_e, rows, 128), F32),
        vmem((n_e, rows, n_o), BF16),
        vmem((rows, n_o), F32),
        vmem((rows, n_i), F32),
        vmem((rows, 128), F32),
        vmem((2, n_z, 2) + cblk, BF16),
        vmem((2, n_z) + cblk, BF16),
        vmem((2, 2, steps) + cblk, BF16),
        vmem(cblk, BF16),
        vmem((2, n_z, 2) + fblk, BF16),
        vmem((2, n_z) + fblk, BF16),
        vmem((2, 2, steps) + fblk, BF16),
        vmem(fblk, BF16),
        pltpu.SemaphoreType.DMA((7,)),
        pltpu.SemaphoreType.DMA((ids.count,)),
        pltpu.SemaphoreType.DMA((ids.count,)),
    ]
    sds = jax.ShapeDtypeStruct
    outs = pl.pallas_call(
        functools.partial(kernel, n_z, n_cores),
        out_shape=(
            sds((rows, width), BF16),
            sds((rows, width), BF16),
            sds(cblk, F32),
            sds((i_rows, width), F32),
            sds((g_rows, width), F32),
            sds((i_rows, width), F32),
            sds((g_rows, n_e), F32),
        ),
        in_specs=[pl.BlockSpec(memory_space=pl.ANY)] * 7,
        out_specs=[pl.BlockSpec(memory_space=pltpu.VMEM)] * 7,
        scratch_shapes=scratch,
        compiler_params=pltpu.CompilerParams(
            collective_id=0, has_side_effects=True, vmem_limit_bytes=56 * 1024 * 1024
        ),
    )(tokens, router_weight, expert_factor.T, input_factor, core_in, output_factor, out_grad)
    mixed, tgrad, cgrad, igrad, rgrad, ograd, egrad = outs
    return mixed, tgrad, jnp.transpose(cgrad, (1, 0, 2)), igrad, rgrad, ograd, egrad


def solution(mesh):
    return jax.shard_map(
        functools.partial(shards, mesh.shape["dp"], mesh.shape["cores"]),
        mesh=mesh,
        in_specs=(
            P("dp", "cores"),
            P(None, "cores"),
            P(None, "cores"),
            P(None, "cores"),
            P("dp", "cores", None),
            P(None, "cores"),
            P("dp", "cores"),
        ),
        out_specs=(
            P("dp", "cores"),
            P("dp", "cores"),
            P("dp", "cores", None),
            P("dp", "cores"),
            P("dp", "cores"),
            P("dp", "cores"),
            P("dp", "cores"),
        ),
        check_vma=False,
    )
```

time: 682 us -> 118 us (0.17)
  waiting for transfers between devices: 334 us -> 0 us
  blocking collectives: 261 us -> 0 us
  Pallas kernels: 0 us -> 108 us
  matrix products: 44.9 us -> 0 us
  local copies, waits for them, and re-layouts: 24.5 us -> 8.22 us
  between operations: 15 us -> 0.66 us
    reduce_scatter x4 -> x0, waiting for transfers between devices: 258 us -> none  [the longest x1 128 us: shards(): lax.psum_scatter(core_term.reshape(core_term.shape[0], local_experts, out...]
    psum x2 -> x0, blocking collectives: 157 us -> none  [the longest x1 79.3 us: shards(): latent = lax.psum(latent_part, 'cores').astype(jnp.bfloat16)]
    pallas_call x0 -> x1, Pallas kernels: none -> 108 us  [shards(): pl.pallas_call(functools.partial(kernel, n_z, n_cores), out_shape=(sds((r...]
    unnamed x1 -> x0, blocking collectives: 105 us -> none
    psum x1 -> x0, waiting for transfers between devices: 76.5 us -> none  [shards(): lax.psum((logit_part, proj_part, back_part), 'cores')]
    dot_general x18 -> x0, matrix products: 44.9 us -> none  [the longest x1 8.37 us: shards(): jnp.einsum('te,teo->to', mixing, expanded.reshape(row_count, local_expert...]
    unnamed x31 -> x20, local copies, waits for them, and re-layouts: 17.7 us -> 8.22 us
  transfers between devices with their start and end apart: 6 -> 0, of which waited for: 4 -> 0; matrix products, arithmetic and copies ran while one was open for 8% -> 0% of each run, Pallas kernels for 0% -> 0%
where the time goes in v1:
time: 118 us; the launch traced here: 117 us
  Pallas kernels  108 us (92%)
  local copies, waits for them, and re-layouts  8.22 us (7%)
    pallas_call x1, Pallas kernels, shards(): pl.pallas_call(functools.partial(kernel, n_z, n_cores), out_shape=(sds((r...  108 us
    unnamed x20, local copies, waits for them, and re-layouts  8.22 us

profile of v1, /device:TPU:2, one launch (start us, length us, event | category | flops | bytes accessed | tf_op | source)
XLA Modules:
  0.0 116.8 jit_solution(8054377981026810214)
XLA Ops:
  0.6 1.6 %copy.17 = bf16[16,8,512]{2,0,1:T(8,128)(2,1)} copy(bf16[16,8,512]{2,1,0:T(8,128)(2,1)} %param.11) | data formatting | bytes 262144 | tf_op args[4]
  2.2 107.9 %shard_map.126 = (bf16[256,768]{1,0:T(8,128)(2,1)}, bf16[256,768]{1,0:T(8,128)(2,1)}, f32[8,16,512]{2,1,0:T(8,128)}, f32[16,768]{1,0:T(8,128)}, f32[8,768]{1,0:T...) custom-call(bf16[256,768]{1,0:T(8,128)(2,1)} %tok_hbm.1, bf16[256,768]{1,0:T(8,128)(2,1)} %rw_hbm.1, bf16[8,256]{1,0:T(8,128)(2,1)} %bitcast.7, ...), custom_call_target="tpu_custom_call" | custom-call | tf_op jit(solution)/shard_map/pallas_call | solution.py:480
  110.2 0.0 copy-start.1
  110.2 1.9 %copy.15 = f32[16,8,512]{2,1,0:T(8,128)} copy(f32[16,8,512]{2,0,1:T(8,128)} %bitcast.6) | data formatting | bytes 524288
  112.1 0.0 copy-done.1
  112.1 0.0 copy-start
  112.1 0.7 copy.24
  112.8 0.4 copy-done
  113.2 0.0 copy-start.3
  113.2 0.7 copy.25
  113.9 0.1 copy-done.3
  114.0 0.0 copy-start.4
  114.0 0.6 copy.26
  114.6 0.1 copy-done.4
  114.7 0.0 copy-start.2
  114.7 0.6 copy.27
  115.3 0.2 copy-done.2
  115.5 0.0 copy-start.5
  115.5 0.6 copy.28
  116.2 0.1 copy-done.5
  116.2 0.6 copy.29
Async XLA Ops:
  110.2 1.9 %copy-start.1 = (bf16[256,768]{1,0:T(8,128)(2,1)S(1)}, bf16[256,768]{1,0:T(8,128)(2,1)}, u32[]{:S(2)}) copy-start(bf16[256,768]{1,0:T(8,128)(2,1)} %get-tuple-element.35) | copy-start | bytes 1179652
  112.1 1.1 copy-start
  113.2 0.8 copy-start.3
  114.0 0.7 copy-start.4
  114.7 0.8 copy-start.2
  115.5 0.7 copy-start.5

commit v2 on v1

--- a/solution.py
+++ b/solution.py
@@ -38,16 +38,19 @@
         self.gather_z = self.take(4 * steps)
         self.gather_sib = self.take(2 * n_z)
         self.factor = self.take(n_cores - 1)
-        self.sum_in = self.take(n_cores - 1)
-        self.share_in = self.take(n_cores - 1)
-        self.sum_mid = self.take(n_cores - 1)
-        self.share_mid = self.take(n_cores - 1)
+        self.sum_in = self.take(2 * (n_cores - 1))
+        self.share_in = self.take(2 * (n_cores - 1))
+        self.sum_mid = self.take(2 * (n_cores - 1))
+        self.share_mid = self.take(2 * (n_cores - 1))
         self.core_sib = self.take(n_e)
         self.core_z = self.take(4 * steps)
         self.core_y = self.take(1)
-        self.fac_sib = self.take(1)
-        self.fac_z = self.take(4 * steps)
-        self.fac_y = self.take(1)
+        self.out_sib = self.take(1)
+        self.out_z = self.take(4 * steps)
+        self.out_y = self.take(1)
+        self.inp_sib = self.take(1)
+        self.inp_z = self.take(4 * steps)
+        self.inp_y = self.take(1)
 
     def take(self, n):
         first = self.count
@@ -59,12 +62,14 @@
     n_z, n_cores,
     tok_hbm, rw_hbm, ef_hbm, inf_hbm, core_hbm, outf_hbm, og_hbm,
     mixed_ref, tgrad_ref, cgrad_ref, igrad_ref, rgrad_ref, ograd_ref, egrad_ref,
-    tok, rw, ef, inf, outf, og,
+    mixed_v, tgrad_v, cgrad_v, igrad_v, rgrad_v, ograd_v, egrad_v,
+    tok, rw, ef, inf, outf, og, core_v,
     whole, ef_all, part_in, got_in, held_in, gates, part_mid, got_mid, held_mid,
     mix_b, outer, lat_acc, pg_acc, mg_acc,
     core_b, core_s, core_r, core_yr,
     fac_b, fac_s, fac_r, fac_yr,
-    in_sem, ss, rs,
+    inp_b, inp_s, inp_r, inp_yr,
+    in_sem, out_sem, ss, rs,
 ):
     rows, width = tok.shape
     n_g = rw.shape[0]
@@ -122,11 +127,11 @@
         pltpu.make_async_copy(src, dst, in_sem.at[n])
         for n, (src, dst) in enumerate(
             (
-                (core_hbm, whole.at[y, z, core]),
+                (core_hbm, core_v),
+                (og_hbm, og),
+                (outf_hbm, outf),
                 (tok_hbm, tok),
                 (inf_hbm, inf),
-                (og_hbm, og),
-                (outf_hbm, outf),
                 (rw_hbm, rw),
                 (ef_hbm, ef),
             )
@@ -139,6 +144,8 @@
     greet = [sib, ynb, znb[0], znb[1]] + peers
     for dev in greet:
         pl.semaphore_signal(barrier, inc=1, device_id=dev, device_id_type=MESH)
+    loads[0].wait()
+    whole[y, z, core] = jnp.swapaxes(core_v[...].astype(F32), 0, 1).astype(BF16)
     pl.semaphore_wait(barrier, len(greet))
 
     lane_y = (y, 1 - y)
@@ -176,55 +183,80 @@
                 ref = whole.at[lane_y[lane], zmod(offset), 1 - core]
                 arrive(ids.gather_sib + lane * n_z + offset, ref)
 
-    loads[0].wait()
+    behind = peers_from(y_hi, x, n_x)
+    n_peers = n_cores - 1
+
+    def sum_send(first, src, got, cols):
+        for k, dev in enumerate(peers):
+            send(first + k, src.at[dev[1], :, cols], got.at[k, :, cols], dev)
+
+    def sum_wait(first, src, got, cols):
+        for k in range(n_peers):
+            arrive(first + k, got.at[k, :, cols])
+        total = src[c, :, cols].astype(F32)
+        for k in range(n_peers):
+            total = total + got[k, :, cols].astype(F32)
+        return total
+
+    def share_send(first, held, cols):
+        for k, dev in enumerate(peers):
+            send(first + k, held.at[c, :, cols], held.at[c, :, cols], dev)
+
+    def share_wait(first, held, cols):
+        for k in range(n_peers):
+            arrive(first + k, held.at[behind[k], :, cols])
+
     send(ids.gather_y, ag_ref(0, z), ag_ref(0, z), ynb)
     ag_open(0)
 
+    n_gi = n_g + n_i
+    gi = slice(0, n_gi)
+    out_cols = slice(n_gi, n_gi + n_o)
+    loads[1].wait()
+    loads[2].wait()
+    part_in[:, :, out_cols] = dot_nt(og[...], outf[...]).reshape(n_cores, block, n_o)
+    sum_send(ids.sum_in, part_in, got_in, out_cols)
+    loads[3].wait()
+    loads[4].wait()
+    part_in[:, :, n_g:n_gi] = dot_nt(tok[...], inf[...]).reshape(n_cores, block, n_i)
+    loads[5].wait()
+    part_in[:, :, :n_g] = dot_nt(tok[...], rw[...]).reshape(n_cores, block, n_g)
+    sum_send(ids.sum_in + n_peers, part_in, got_in, gi)
     loads[6].wait()
     ef_all[c] = ef[...].astype(F32)
     for k, dev in enumerate(peers):
         send(ids.factor + k, ef_all.at[c], ef_all.at[c], dev)
-    loads[1].wait()
-    loads[2].wait()
-    part_in[:, :, n_g : n_g + n_i] = (
-        dot_nt(tok[...], inf[...]).reshape(n_cores, block, n_i)
-    )
-    loads[3].wait()
-    loads[4].wait()
-    part_in[:, :, n_g + n_i :] = (
-        dot_nt(og[...], outf[...]).reshape(n_cores, block, n_o)
-    )
-    loads[5].wait()
-    part_in[:, :, :n_g] = dot_nt(tok[...], rw[...]).reshape(n_cores, block, n_g)
-    for k, dev in enumerate(peers):
-        send(ids.sum_in + k, part_in.at[dev[1]], got_in.at[k], dev)
 
     arrive(ids.gather_y, ag_ref(1, z))
     ag_open(1)
     ag_step(1, 0)
-
-    for k in range(n_cores - 1):
-        arrive(ids.sum_in + k, got_in.at[k])
-    total = part_in[c]
-    for k in range(n_cores - 1):
-        total = total + got_in[k]
+    ag_step(1, 1)
+
+    held_in[c, :, out_cols] = sum_wait(ids.sum_in, part_in, got_in, out_cols).astype(BF16)
+    share_send(ids.share_in, held_in, out_cols)
+
+    ag_step(2, 0)
+    ag_step(2, 1)
+    ag_step(3, 0)
+
+    total = sum_wait(ids.sum_in + n_peers, part_in, got_in, gi)
     gate = jax.nn.sigmoid(total[:, :n_g])
     gates[...] = gate
     held_in[c, :, :n_g] = gate.astype(BF16)
-    held_in[c, :, n_g:] = total[:, n_g:].astype(BF16)
-    for k, dev in enumerate(peers):
-        send(ids.share_in + k, held_in.at[c], held_in.at[c], dev)
-
-    ag_step(1, 1)
-    ag_step(2, 0)
-
-    for k in range(n_cores - 1):
-        ref = held_in.at[peers_from(y_hi, x, n_x)[k]]
-        arrive(ids.share_in + k, ref)
-
+    held_in[c, :, n_g:n_gi] = total[:, n_g:].astype(BF16)
+    share_send(ids.share_in + n_peers, held_in, gi)
+
+    ag_step(3, 1)
+    for s in range(4, steps + 1):
+        ag_step(s, 0)
+        ag_step(s, 1)
+
+    share_wait(ids.share_in, held_in, out_cols)
+    lgrad = held_in[:, :, out_cols].reshape(rows, n_o)
+    lgrad_wide = lgrad.astype(F32)
+    share_wait(ids.share_in + n_peers, held_in, gi)
     gate_low = held_in[:, :, :n_g].reshape(rows, n_g)
-    proj = held_in[:, :, n_g : n_g + n_i].reshape(rows, n_i)
-    lgrad = held_in[:, :, n_g + n_i :].reshape(rows, n_o)
+    proj = held_in[:, :, n_g:n_gi].reshape(rows, n_i)
     mixing = dot_nt(gate_low, ef[...])
     for e in range(n_e):
         mix_b[e] = jnp.broadcast_to(mixing[:, e : e + 1], (rows, 128))
@@ -233,29 +265,26 @@
         return jnp.concatenate([v] * (n // 128), axis=1)
 
     proj_t = proj.T
-    lgrad_wide = lgrad.astype(F32)
-
-    def core_terms(e, _):
-        o = (wide(mix_b[e], n_o) * lgrad_wide).astype(BF16)
-        outer[e] = o
-        term = dot_nn(proj_t, o) * inv_rows
-        core_b[:, :, :, e] = term.astype(BF16).reshape(2, n_z, 2, i_rows, n_o)
-        pltpu.make_async_remote_copy(
+
+    def core_sib(e):
+        return pltpu.make_async_remote_copy(
             core_b.at[:, :, 1 - core, e],
             core_s.at[:, :, e],
             ss.at[ids.core_sib + e],
             rs.at[ids.core_sib + e],
             device_id=sib,
             device_id_type=MESH,
-        ).start()
+        )
+
+    def core_terms(e, _):
+        o = (wide(mix_b[e], n_o) * lgrad_wide).astype(BF16)
+        outer[e] = o
+        term = dot_nn(proj_t, o) * inv_rows
+        core_b[:, :, :, e] = term.astype(BF16).reshape(2, n_z, 2, i_rows, n_o)
+        core_sib(e).start()
         return 0
 
     lax.fori_loop(0, n_e, core_terms, 0)
-
-    ag_step(2, 1)
-    for s in range(3, steps + 1):
-        ag_step(s, 0)
-        ag_step(s, 1)
 
     def rs_step(s, src, sib_got, got, first):
         for lane in range(2):
@@ -298,11 +327,8 @@
         return val + yr[...].astype(F32)
 
     core_args = (core_b, core_s, core_r)
-    fac_args = (fac_b, fac_s, fac_r)
-
-    for e in range(n_e):
-        arrive(ids.core_sib + e, core_s.at[:, :, e])
-    rs_step(1, *core_args, ids.core_z)
+    fac_o = (fac_b, fac_s, fac_r)
+    fac_i = (inp_b, inp_s, inp_r)
 
     ag_close()
 
@@ -311,109 +337,146 @@
     mg_acc[...] = jnp.zeros_like(mg_acc)
     lane_no = lax.broadcasted_iota(jnp.int32, (rows, 128), 1)
 
-    def middle(e, _):
-        core_e = whole[:, :, :, e].reshape(n_i, n_o)
-        expanded = dot_nn(proj, core_e)
+    def forward(e, _):
+        expanded = dot_nn(proj, whole[:, :, :, e].reshape(n_i, n_o))
         lat_acc[...] += wide(mix_b[e], n_o) * expanded
         col = jnp.sum(lgrad_wide * expanded, axis=1, keepdims=True)
         mg_acc[...] += jnp.where(lane_no == c * n_e + e, col, 0.0)
-        pg_acc[...] += dot_nt(outer[e], core_e)
         return 0
 
-    lax.fori_loop(0, n_e, middle, 0)
-
+    def backward(e, _):
+        pg_acc[...] += dot_nt(outer[e], whole[:, :, :, e].reshape(n_i, n_o))
+        return 0
+
+    n_om = n_o + 128
+    lat_mix = slice(0, n_om)
+    pg_cols = slice(n_om, n_om + n_i)
+    lax.fori_loop(0, n_e, forward, 0)
     part_mid[:, :, :n_o] = lat_acc[...].astype(BF16).reshape(n_cores, block, n_o)
-    part_mid[:, :, n_o : n_o + n_i] = pg_acc[...].astype(BF16).reshape(n_cores, block, n_i)
     mix_low = mg_acc[...].astype(BF16)
-    part_mid[:, :, n_o + n_i :] = mix_low.reshape(n_cores, block, 128)
-    for k, dev in enumerate(peers):
-        send(ids.sum_mid + k, part_mid.at[dev[1]], got_mid.at[k], dev)
-
-    expert_full = lax.dot_general(
-        gate_low, mix_low, (((0,), (0,)), ((), ())), preferred_element_type=F32
-    ) * inv_rows
+    part_mid[:, :, n_o:n_om] = mix_low.reshape(n_cores, block, 128)
+    sum_send(ids.sum_mid, part_mid, got_mid, lat_mix)
+
+    for e in range(n_e):
+        arrive(ids.core_sib + e, core_s.at[:, :, e])
+    rs_step(1, *core_args, ids.core_z)
+
+    lax.fori_loop(0, n_e, backward, 0)
+    part_mid[:, :, pg_cols] = pg_acc[...].astype(BF16).reshape(n_cores, block, n_i)
+    sum_send(ids.sum_mid + n_peers, part_mid, got_mid, pg_cols)
+
+    expert_full = dot_tn(gate_low, mix_low) * inv_rows
     pick = (
         lax.broadcasted_iota(jnp.int32, (128, 128), 0)
         == lax.broadcasted_iota(jnp.int32, (128, 128), 1) + c * n_e
     ).astype(BF16)
     expert_term = dot_nn(expert_full.astype(BF16), pick)
 
-    rs_step(2, *core_args, ids.core_z)
-
-    for k in range(n_cores - 1):
-        arrive(ids.factor + k, ef_all.at[peers_from(y_hi, x, n_x)[k]])
-    for k in range(n_cores - 1):
-        arrive(ids.sum_mid + k, got_mid.at[k])
-    total = part_mid[c].astype(F32)
-    for k in range(n_cores - 1):
-        total = total + got_mid[k].astype(F32)
-    mix_block = total[:, n_o + n_i : n_o + n_i + n_cores * n_e].astype(BF16)
+    for k in range(n_peers):
+        arrive(ids.factor + k, ef_all.at[behind[k]])
+    total = sum_wait(ids.sum_mid, part_mid, got_mid, lat_mix)
+    mix_block = total[:, n_o : n_o + n_cores * n_e].astype(BF16)
     gate_grad = dot_nn(mix_block, ef_all[...].reshape(n_cores * n_e, n_g).astype(BF16))
     gate = gates[...]
-    held_mid[c, :, : n_o + n_i] = total[:, : n_o + n_i].astype(BF16)
-    held_mid[c, :, n_o + n_i :] = (gate_grad * gate * (1.0 - gate)).astype(BF16)
-    for k, dev in enumerate(peers):
-        send(ids.share_mid + k, held_mid.at[c], held_mid.at[c], dev)
-
-    rs_step(3, *core_args, ids.core_z)
-
-    for k in range(n_cores - 1):
-        arrive(ids.share_mid + k, held_mid.at[peers_from(y_hi, x, n_x)[k]])
+    n_og = n_o + n_g
+    lat_logit = slice(0, n_og)
+    pg_held = slice(n_og, n_og + n_i)
+    held_mid[c, :, :n_o] = total[:, :n_o].astype(BF16)
+    held_mid[c, :, n_o:n_og] = (gate_grad * gate * (1.0 - gate)).astype(BF16)
+    share_send(ids.share_mid, held_mid, lat_logit)
+
+    rs_step(2, *core_args, ids.core_z)
+
+    held_mid[c, :, pg_held] = sum_wait(
+        ids.sum_mid + n_peers, part_mid, got_mid, pg_cols
+    ).astype(BF16)
+    share_send(ids.share_mid + n_peers, held_mid, pg_held)
+
+    share_wait(ids.share_mid, held_mid, lat_logit)
     latent = held_mid[:, :, :n_o].reshape(rows, n_o)
-    pgrad = held_mid[:, :, n_o : n_o + n_i].reshape(rows, n_i)
-    logit_grad = held_mid[:, :, n_o + n_i :].reshape(rows, n_g)
+    logit_grad = held_mid[:, :, n_o:n_og].reshape(rows, n_g)
     blk = (2, n_z, 2)
+    g_rows = n_g // n_dp
     fac_b[:, :, :, :i_rows] = (
-        (dot_tn(pgrad, tok[...]) * inv_rows).astype(BF16).reshape(*blk, i_rows, width)
-    )
-    fac_b[:, :, :, i_rows : 2 * i_rows] = (
         (dot_tn(latent, og[...]) * inv_rows).astype(BF16).reshape(*blk, i_rows, width)
     )
-    g_rows = n_g // n_dp
     router_term = (dot_tn(logit_grad, tok[...]) * inv_rows).reshape(*blk, g_rows, width)
     expert_wide = jnp.concatenate(
         [expert_term, jnp.zeros((n_g, width - 128), F32)], axis=1
     ) if width > 128 else expert_term
-    fac_b[:, :, :, 2 * i_rows :] = jnp.concatenate(
+    fac_b[:, :, :, i_rows:] = jnp.concatenate(
         [router_term, expert_wide.reshape(*blk, g_rows, width)], axis=3
     ).astype(BF16)
-    send(ids.fac_sib, fac_b.at[:, :, 1 - core], fac_s, sib)
-
-    rs_step(4, *core_args, ids.core_z)
-    for s in range(5, steps + 1):
+    send(ids.out_sib, fac_b.at[:, :, 1 - core], fac_s, sib)
+
+    rs_step(3, *core_args, ids.core_z)
+
+    arrive(ids.out_sib, fac_s)
+    rs_step(1, *fac_o, ids.out_z)
+
+    share_wait(ids.share_mid + n_peers, held_mid, pg_held)
+    pgrad = held_mid[:, :, pg_held].reshape(rows, n_i)
+    inp_b[...] = (dot_tn(pgrad, tok[...]) * inv_rows).astype(BF16).reshape(*blk, i_rows, width)
+    send(ids.inp_sib, inp_b.at[:, :, 1 - core], inp_s, sib)
+
+    for s in range(4, steps + 1):
         rs_step(s, *core_args, ids.core_z)
-
-    arrive(ids.fac_sib, fac_s)
-    rs_step(1, *fac_args, ids.fac_z)
+    arrive(ids.inp_sib, inp_s)
+    rs_step(1, *fac_i, ids.inp_z)
+    rs_step(2, *fac_o, ids.out_z)
+
+    mixed_v[...] = dot_nn(latent, outf[...]).astype(BF16)
+    results = [pltpu.make_async_copy(mixed_v, mixed_ref, out_sem.at[0])]
+    results[0].start()
+
     rs_turn(*core_args, core_yr, ids.core_z, ids.core_y)
-    mixed_ref[...] = dot_nn(latent, outf[...]).astype(BF16)
-    rs_step(2, *fac_args, ids.fac_z)
-    tgrad_ref[...] = (dot_nn(pgrad, inf[...]) + dot_nn(logit_grad, rw[...])).astype(BF16)
-    for s in range(3, steps + 1):
-        rs_step(s, *fac_args, ids.fac_z)
-    cgrad_ref[...] = rs_end(*core_args, core_yr, ids.core_z, ids.core_y)
-    rs_turn(*fac_args, fac_yr, ids.fac_z, ids.fac_y)
-    val = rs_end(*fac_args, fac_yr, ids.fac_z, ids.fac_y)
-    igrad_ref[...] = val[:i_rows]
-    ograd_ref[...] = val[i_rows : 2 * i_rows]
-    rgrad_ref[...] = val[2 * i_rows : 2 * i_rows + g_rows]
-    egrad_ref[...] = val[2 * i_rows + g_rows :, :n_e]
+    rs_step(2, *fac_i, ids.inp_z)
+    rs_step(3, *fac_o, ids.out_z)
+    tgrad_v[...] = (dot_nn(pgrad, inf[...]) + dot_nn(logit_grad, rw[...])).astype(BF16)
+
+    def result(src, dst):
+        results.append(pltpu.make_async_copy(src, dst, out_sem.at[len(results)]))
+        results[-1].start()
+
+    result(tgrad_v, tgrad_ref)
+    rs_step(3, *fac_i, ids.inp_z)
+    for s in range(4, steps + 1):
+        rs_step(s, *fac_o, ids.out_z)
+        rs_step(s, *fac_i, ids.inp_z)
+    rs_turn(*fac_o, fac_yr, ids.out_z, ids.out_y)
+    rs_turn(*fac_i, inp_yr, ids.inp_z, ids.inp_y)
+    cgrad_v[...] = jnp.swapaxes(rs_end(*core_args, core_yr, ids.core_z, ids.core_y), 0, 1)
+    result(cgrad_v, cgrad_ref)
+    val = rs_end(*fac_o, fac_yr, ids.out_z, ids.out_y)
+    ograd_v[...] = val[:i_rows]
+    rgrad_v[...] = val[i_rows : i_rows + g_rows]
+    egrad_v[...] = val[i_rows + g_rows :, :n_e]
+    result(ograd_v, ograd_ref)
+    result(rgrad_v, rgrad_ref)
+    result(egrad_v, egrad_ref)
+    igrad_v[...] = rs_end(*fac_i, inp_yr, ids.inp_z, ids.inp_y)
+    result(igrad_v, igrad_ref)
 
     for d in sent:
         d.wait_send()
 
     def drain(e, _):
-        pltpu.make_async_remote_copy(
-            core_b.at[:, :, 1 - core, e],
-            core_s.at[:, :, e],
-            ss.at[ids.core_sib + e],
-            rs.at[ids.core_sib + e],
-            device_id=sib,
-            device_id_type=MESH,
-        ).wait_send()
+        core_sib(e).wait_send()
         return 0
 
     lax.fori_loop(0, n_e, drain, 0)
+    for r in results:
+        r.wait()
+
+
+def hand_over(*refs):
+    n = len(refs) // 2
+    sems = refs[-1]
+    copies = [pltpu.make_async_copy(refs[i], refs[n + i], sems.at[i]) for i in range(n)]
+    for copy in copies:
+        copy.start()
+    for copy in copies:
+        copy.wait()
 
 
 def peers_from(y_hi, x, n_x):
@@ -436,20 +499,31 @@
     i_rows, n_e, _ = core_tensor.shape
     g_rows = n_g // n_dp
     block = rows // n_cores
-    core_in = jnp.transpose(core_tensor, (1, 0, 2))
     cblk = (n_e, i_rows, n_o)
-    fblk = (2 * i_rows + 2 * g_rows, width)
+    fblk = (i_rows + 2 * g_rows, width)
+    iblk = (i_rows, width)
     in_cols = n_g + n_i + n_o
     mid_cols = n_o + n_i + 128
     ids = Ids(n_z, n_cores, n_e)
+    sds = jax.ShapeDtypeStruct
+    results = (
+        sds((rows, width), BF16),
+        sds((rows, width), BF16),
+        sds((i_rows, n_e, n_o), F32),
+        sds((i_rows, width), F32),
+        sds((g_rows, width), F32),
+        sds((i_rows, width), F32),
+        sds((g_rows, n_e), F32),
+    )
     vmem = pltpu.VMEM
-    scratch = [
+    scratch = [vmem(r.shape, r.dtype) for r in results] + [
         vmem((rows, width), BF16),
         vmem((n_g, width), BF16),
         vmem((n_e, n_g), BF16),
         vmem((n_i, width), BF16),
         vmem((n_o, width), BF16),
         vmem((rows, width), BF16),
+        vmem((i_rows, n_e, n_o), BF16),
         vmem((2, n_z, 2) + cblk, BF16),
         vmem((n_cores, n_e, n_g), F32),
         vmem((n_cores, block, in_cols), F32),
@@ -472,31 +546,32 @@
         vmem((2, n_z) + fblk, BF16),
         vmem((2, 2, steps) + fblk, BF16),
         vmem(fblk, BF16),
+        vmem((2, n_z, 2) + iblk, BF16),
+        vmem((2, n_z) + iblk, BF16),
+        vmem((2, 2, steps) + iblk, BF16),
+        vmem(iblk, BF16),
+        pltpu.SemaphoreType.DMA((7,)),
         pltpu.SemaphoreType.DMA((7,)),
         pltpu.SemaphoreType.DMA((ids.count,)),
         pltpu.SemaphoreType.DMA((ids.count,)),
     ]
-    sds = jax.ShapeDtypeStruct
     outs = pl.pallas_call(
         functools.partial(kernel, n_z, n_cores),
-        out_shape=(
-            sds((rows, width), BF16),
-            sds((rows, width), BF16),
-            sds(cblk, F32),
-            sds((i_rows, width), F32),
-            sds((g_rows, width), F32),
-            sds((i_rows, width), F32),
-            sds((g_rows, n_e), F32),
-        ),
+        out_shape=results,
         in_specs=[pl.BlockSpec(memory_space=pl.ANY)] * 7,
-        out_specs=[pl.BlockSpec(memory_space=pltpu.VMEM)] * 7,
+        out_specs=[pl.BlockSpec(memory_space=pl.ANY)] * 7,
         scratch_shapes=scratch,
         compiler_params=pltpu.CompilerParams(
             collective_id=0, has_side_effects=True, vmem_limit_bytes=56 * 1024 * 1024
         ),
-    )(tokens, router_weight, expert_factor.T, input_factor, core_in, output_factor, out_grad)
-    mixed, tgrad, cgrad, igrad, rgrad, ograd, egrad = outs
-    return mixed, tgrad, jnp.transpose(cgrad, (1, 0, 2)), igrad, rgrad, ograd, egrad
+    )(tokens, router_weight, expert_factor.T, input_factor, core_tensor, output_factor, out_grad)
+    return pl.pallas_call(
+        hand_over,
+        out_shape=results,
+        in_specs=[pl.BlockSpec(memory_space=pl.ANY)] * 7,
+        out_specs=[pl.BlockSpec(memory_space=pl.ANY)] * 7,
+        scratch_shapes=[pltpu.SemaphoreType.DMA((7,))],
+    )(*outs)
 
 
 def solution(mesh):

time: 118 us -> 128 us (1.085)
  Pallas kernels: 108 us -> 127 us
  local copies, waits for them, and re-layouts: 8.22 us -> 0 us
    pallas_call x1 -> x2, Pallas kernels: 108 us -> 127 us  [the longest x1 90 us: shards(): pl.pallas_call(functools.partial(kernel, n_z, n_cores), out_shape=results...]
    unnamed x20 -> x0, local copies, waits for them, and re-layouts: 8.22 us -> none
where the time goes in v2:
time: 128 us; the launch traced here: 127 us
  Pallas kernels  127 us (99%)
    pallas_call x1, Pallas kernels, shards(): pl.pallas_call(functools.partial(kernel, n_z, n_cores), out_shape=results...  90 us
    pallas_call x1, Pallas kernels, shards(): pl.pallas_call(hand_over, out_shape=results, in_specs=[pl.BlockSpec(memor...  36.8 us

profile of v2, /device:TPU:2, one launch (start us, length us, event | category | flops | bytes accessed | tf_op | source)
XLA Modules:
  0.0 127.4 jit_solution(13673273923335132599)
XLA Ops:
  0.6 90.0 %shard_map.126 = (bf16[256,768]{1,0:T(8,128)(2,1)}, bf16[256,768]{1,0:T(8,128)(2,1)}, f32[16,8,512]{2,1,0:T(8,128)}, f32[16,768]{1,0:T(8,128)}, f32[8,768]{1,0:T...) custom-call(bf16[256,768]{1,0:T(8,128)(2,1)} %tok_hbm.1, bf16[256,768]{1,0:T(8,128)(2,1)} %rw_hbm.1, bf16[8,256]{1,0:T(8,128)(2,1)} %bitcast.1, ...), custom_call_target="tpu_custom_call" | custom-call | tf_op jit(solution)/shard_map/pallas_call | solution.py:558
  90.6 36.8 %shard_map.127 = (bf16[256,768]{1,0:T(8,128)(2,1)}, bf16[256,768]{1,0:T(8,128)(2,1)}, f32[16,8,512]{2,1,0:T(8,128)}, f32[16,768]{1,0:T(8,128)}, f32[8,768]{1,0:T...) custom-call(bf16[256,768]{1,0:T(8,128)(2,1)} %get-tuple-element.14.refs_0_, bf16[256,768]{1,0:T(8,128)(2,1)} %get-tuple-element.15.refs_1_, ...), custom_call_target="tpu_custom_call" | custom-call | tf_op jit(solution)/shard_map/pallas_call | solution.py:568

commit v3 on v2

--- a/solution.py
+++ b/solution.py
@@ -469,13 +469,17 @@
         r.wait()
 
 
-def hand_over(*refs):
-    n = len(refs) // 2
-    sems = refs[-1]
-    copies = [pltpu.make_async_copy(refs[i], refs[n + i], sems.at[i]) for i in range(n)]
-    for copy in copies:
+def hand_over(n, *refs):
+    srcs, dsts, held = refs[:n], refs[n : 2 * n], refs[2 * n : 3 * n]
+    in_sem, out_sem = refs[3 * n :]
+    ins = [pltpu.make_async_copy(srcs[i], held[i], in_sem.at[i]) for i in range(n)]
+    outs = [pltpu.make_async_copy(held[i], dsts[i], out_sem.at[i]) for i in range(n)]
+    for copy in ins:
         copy.start()
-    for copy in copies:
+    for i in range(n):
+        ins[i].wait()
+        outs[i].start()
+    for copy in outs:
         copy.wait()
 
 
@@ -566,11 +570,12 @@
         ),
     )(tokens, router_weight, expert_factor.T, input_factor, core_tensor, output_factor, out_grad)
     return pl.pallas_call(
-        hand_over,
+        functools.partial(hand_over, len(results)),
         out_shape=results,
         in_specs=[pl.BlockSpec(memory_space=pl.ANY)] * 7,
         out_specs=[pl.BlockSpec(memory_space=pl.ANY)] * 7,
-        scratch_shapes=[pltpu.SemaphoreType.DMA((7,))],
+        scratch_shapes=[vmem(r.shape, r.dtype) for r in results]
+        + [pltpu.SemaphoreType.DMA((7,))] * 2,
     )(*outs)
 
 

time: 128 us -> 93.4 us (0.73)
  Pallas kernels: 127 us -> 92.1 us
    pallas_call x1, Pallas kernels: 36.8 us -> 2.11 us  [shards(): pl.pallas_call(functools.partial(hand_over, len(results)), out_shape=resu...]
where the time goes in v3:
time: 93.4 us; the launch traced here: 92.7 us
  Pallas kernels  92.1 us (99%)
    pallas_call x1, Pallas kernels, shards(): pl.pallas_call(functools.partial(kernel, n_z, n_cores), out_shape=results...  90 us
    pallas_call x1, Pallas kernels, shards(): pl.pallas_call(functools.partial(hand_over, len(results)), out_shape=resu...  2.11 us

profile of v3, /device:TPU:2, one launch (start us, length us, event | category | flops | bytes accessed | tf_op | source)
XLA Modules:
  0.0 92.7 jit_solution(8518214271215950851)
XLA Ops:
  0.6 90.0 %shard_map.126 = (bf16[256,768]{1,0:T(8,128)(2,1)}, bf16[256,768]{1,0:T(8,128)(2,1)}, f32[16,8,512]{2,1,0:T(8,128)}, f32[16,768]{1,0:T(8,128)}, f32[8,768]{1,0:T...) custom-call(bf16[256,768]{1,0:T(8,128)(2,1)} %tok_hbm.1, bf16[256,768]{1,0:T(8,128)(2,1)} %rw_hbm.1, bf16[8,256]{1,0:T(8,128)(2,1)} %bitcast.1, ...), custom_call_target="tpu_custom_call" | custom-call | tf_op jit(solution)/shard_map/pallas_call | solution.py:562
  90.6 2.1 %shard_map.127 = (bf16[256,768]{1,0:T(8,128)(2,1)}, bf16[256,768]{1,0:T(8,128)(2,1)}, f32[16,8,512]{2,1,0:T(8,128)}, f32[16,768]{1,0:T(8,128)}, f32[8,768]{1,0:T...) custom-call(bf16[256,768]{1,0:T(8,128)(2,1)} %get-tuple-element.14.refs_0_, bf16[256,768]{1,0:T(8,128)(2,1)} %get-tuple-element.15.refs_1_, ...), custom_call_target="tpu_custom_call" | custom-call | tf_op jit(solution)/shard_map/pallas_call | solution.py:572

commit v4 on v3

--- a/solution.py
+++ b/solution.py
@@ -42,7 +42,7 @@
         self.share_in = self.take(2 * (n_cores - 1))
         self.sum_mid = self.take(2 * (n_cores - 1))
         self.share_mid = self.take(2 * (n_cores - 1))
-        self.core_sib = self.take(n_e)
+        self.core_sib = self.take(2)
         self.core_z = self.take(4 * steps)
         self.core_y = self.take(1)
         self.out_sib = self.take(1)
@@ -64,9 +64,9 @@
     mixed_ref, tgrad_ref, cgrad_ref, igrad_ref, rgrad_ref, ograd_ref, egrad_ref,
     mixed_v, tgrad_v, cgrad_v, igrad_v, rgrad_v, ograd_v, egrad_v,
     tok, rw, ef, inf, outf, og, core_v,
-    whole, ef_all, part_in, got_in, held_in, gates, part_mid, got_mid, held_mid,
-    mix_b, outer, lat_acc, pg_acc, mg_acc,
-    core_b, core_s, core_r, core_yr,
+    whole, ef_all, part_a, got_a, held_a, part_p, got_p, held_p, gates, part_mid, got_mid, held_mid,
+    mix_b, sib_a, sib_mix, proj_t, sib_pt, lat_acc, pg_acc, mg_acc,
+    core_b, core_r, core_yr,
     fac_b, fac_s, fac_r, fac_yr,
     inp_b, inp_s, inp_r, inp_yr,
     in_sem, out_sem, ss, rs,
@@ -131,8 +131,8 @@
                 (og_hbm, og),
                 (outf_hbm, outf),
                 (tok_hbm, tok),
+                (rw_hbm, rw),
                 (inf_hbm, inf),
-                (rw_hbm, rw),
                 (ef_hbm, ef),
             )
         )
@@ -209,19 +209,18 @@
     send(ids.gather_y, ag_ref(0, z), ag_ref(0, z), ynb)
     ag_open(0)
 
-    n_gi = n_g + n_i
-    gi = slice(0, n_gi)
-    out_cols = slice(n_gi, n_gi + n_o)
+    n_go = n_g + n_o
+    everything = slice(None)
     loads[1].wait()
     loads[2].wait()
-    part_in[:, :, out_cols] = dot_nt(og[...], outf[...]).reshape(n_cores, block, n_o)
-    sum_send(ids.sum_in, part_in, got_in, out_cols)
+    part_a[:, :, n_g:] = dot_nt(og[...], outf[...]).astype(BF16).reshape(n_cores, block, n_o)
     loads[3].wait()
     loads[4].wait()
-    part_in[:, :, n_g:n_gi] = dot_nt(tok[...], inf[...]).reshape(n_cores, block, n_i)
+    part_a[:, :, :n_g] = dot_nt(tok[...], rw[...]).astype(BF16).reshape(n_cores, block, n_g)
+    sum_send(ids.sum_in, part_a, got_a, everything)
     loads[5].wait()
-    part_in[:, :, :n_g] = dot_nt(tok[...], rw[...]).reshape(n_cores, block, n_g)
-    sum_send(ids.sum_in + n_peers, part_in, got_in, gi)
+    part_p[...] = dot_nt(tok[...], inf[...]).reshape(n_cores, block, n_i)
+    sum_send(ids.sum_in + n_peers, part_p, got_p, everything)
     loads[6].wait()
     ef_all[c] = ef[...].astype(F32)
     for k, dev in enumerate(peers):
@@ -232,104 +231,124 @@
     ag_step(1, 0)
     ag_step(1, 1)
 
-    held_in[c, :, out_cols] = sum_wait(ids.sum_in, part_in, got_in, out_cols).astype(BF16)
-    share_send(ids.share_in, held_in, out_cols)
+    total = sum_wait(ids.sum_in, part_a, got_a, everything)
+    gate = jax.nn.sigmoid(total[:, :n_g])
+    gates[...] = gate
+    held_a[c, :, :n_g] = gate.astype(BF16)
+    held_a[c, :, n_g:] = total[:, n_g:].astype(BF16)
+    share_send(ids.share_in, held_a, everything)
 
     ag_step(2, 0)
+
+    held_p[c] = sum_wait(ids.sum_in + n_peers, part_p, got_p, everything).astype(BF16)
+    share_send(ids.share_in + n_peers, held_p, everything)
+
     ag_step(2, 1)
     ag_step(3, 0)
 
-    total = sum_wait(ids.sum_in + n_peers, part_in, got_in, gi)
-    gate = jax.nn.sigmoid(total[:, :n_g])
-    gates[...] = gate
-    held_in[c, :, :n_g] = gate.astype(BF16)
-    held_in[c, :, n_g:n_gi] = total[:, n_g:].astype(BF16)
-    share_send(ids.share_in + n_peers, held_in, gi)
+    def wide(v, n):
+        return jnp.concatenate([v] * (n // 128), axis=1)
+
+    def spread_mixing(held, out):
+        mixing = dot_nt(held[:, :, :n_g].reshape(rows, n_g), ef[...])
+        for e in range(n_e):
+            out[e] = jnp.broadcast_to(mixing[:, e : e + 1], (rows, 128))
+
+    share_wait(ids.share_in, held_a, everything)
+    send(ids.core_sib, held_a, sib_a, sib)
+    spread_mixing(held_a, mix_b)
+    lgrad = held_a[:, :, n_g:].reshape(rows, n_o)
+    lgrad_wide = lgrad.astype(F32)
 
     ag_step(3, 1)
+
+    share_wait(ids.share_in + n_peers, held_p, everything)
+    proj = held_p[...].reshape(rows, n_i)
+    proj_t[...] = proj.T.reshape(2 * n_z, 2, i_rows, rows)
+    send(ids.core_sib + 1, proj_t.at[:, 1 - core], sib_pt, sib)
+    arrive(ids.core_sib, sib_a)
+    spread_mixing(sib_a, sib_mix)
+    sib_lgrad = sib_a[:, :, n_g:].reshape(rows, n_o).astype(F32)
+    half = 2 * n_z * i_rows
+    own_t = proj_t[:, core].reshape(half, rows)
+    arrive(ids.core_sib + 1, sib_pt)
+    sib_t = sib_pt[...].reshape(half, rows)
+
+    def core_terms(e, _):
+        own = (wide(mix_b[e], n_o) * lgrad_wide).astype(BF16)
+        other = (wide(sib_mix[e], n_o) * sib_lgrad).astype(BF16)
+        term = (dot_nn(own_t, own) + dot_nn(sib_t, other)) * inv_rows
+        core_b[:, :, e] = term.astype(BF16).reshape(2, n_z, i_rows, n_o)
+        return 0
+
+    lax.fori_loop(0, n_e, core_terms, 0)
+
+    def rs_ring(block_of, sib_of, got, yr, z_id, y_id):
+        def num(lane, way, s):
+            return z_id + (lane * 2 + way) * steps + s - 1
+
+        def base(lane, d):
+            val = block_of(lane_y[lane], d)[...].astype(F32)
+            if sib_of is not None:
+                val = val + sib_of(lane_y[lane], d)[...].astype(F32)
+            return val
+
+        def step(s):
+            for lane in range(2):
+                for way in range(2):
+                    k = hops[lane][way]
+                    if s <= k:
+                        far = k - s + 1
+                        d = zmod(far if way == 0 else -far)
+                        out = block_of(lane_y[lane], d)
+                        if s > 1:
+                            arrive(num(lane, way, s - 1), got.at[lane, way, s - 2])
+                            val = base(lane, d) + got[lane, way, s - 2].astype(F32)
+                            out[...] = val.astype(BF16)
+                        elif sib_of is not None:
+                            out[...] = base(lane, d).astype(BF16)
+                        send(num(lane, way, s), out, got.at[lane, way, s - 1], znb[way])
+
+        def lane_sum(lane):
+            val = base(lane, z)
+            for way in range(2):
+                k = hops[lane][way]
+                if k:
+                    arrive(num(lane, way, k), got.at[lane, way, k - 1])
+                    val = val + got[lane, way, k - 1].astype(F32)
+            return val
+
+        def turn():
+            val = lane_sum(1)
+            out = block_of(1 - y, z)
+            out[...] = val.astype(BF16)
+            send(y_id, out, yr, ynb)
+
+        def end():
+            val = lane_sum(0)
+            arrive(y_id, yr)
+            return val + yr[...].astype(F32)
+
+        return step, turn, end
+
+    core_step, core_turn, core_end = rs_ring(
+        lambda yy, d: core_b.at[yy, d], None, core_r, core_yr, ids.core_z, ids.core_y
+    )
+    out_step, out_turn, out_end = rs_ring(
+        lambda yy, d: fac_b.at[yy, d, core],
+        lambda yy, d: fac_s.at[yy, d],
+        fac_r, fac_yr, ids.out_z, ids.out_y,
+    )
+    inp_step, inp_turn, inp_end = rs_ring(
+        lambda yy, d: inp_b.at[yy, d, core],
+        lambda yy, d: inp_s.at[yy, d],
+        inp_r, inp_yr, ids.inp_z, ids.inp_y,
+    )
+
+    core_step(1)
     for s in range(4, steps + 1):
         ag_step(s, 0)
         ag_step(s, 1)
-
-    share_wait(ids.share_in, held_in, out_cols)
-    lgrad = held_in[:, :, out_cols].reshape(rows, n_o)
-    lgrad_wide = lgrad.astype(F32)
-    share_wait(ids.share_in + n_peers, held_in, gi)
-    gate_low = held_in[:, :, :n_g].reshape(rows, n_g)
-    proj = held_in[:, :, n_g:n_gi].reshape(rows, n_i)
-    mixing = dot_nt(gate_low, ef[...])
-    for e in range(n_e):
-        mix_b[e] = jnp.broadcast_to(mixing[:, e : e + 1], (rows, 128))
-
-    def wide(v, n):
-        return jnp.concatenate([v] * (n // 128), axis=1)
-
-    proj_t = proj.T
-
-    def core_sib(e):
-        return pltpu.make_async_remote_copy(
-            core_b.at[:, :, 1 - core, e],
-            core_s.at[:, :, e],
-            ss.at[ids.core_sib + e],
-            rs.at[ids.core_sib + e],
-            device_id=sib,
-            device_id_type=MESH,
-        )
-
-    def core_terms(e, _):
-        o = (wide(mix_b[e], n_o) * lgrad_wide).astype(BF16)
-        outer[e] = o
-        term = dot_nn(proj_t, o) * inv_rows
-        core_b[:, :, :, e] = term.astype(BF16).reshape(2, n_z, 2, i_rows, n_o)
-        core_sib(e).start()
-        return 0
-
-    lax.fori_loop(0, n_e, core_terms, 0)
-
-    def rs_step(s, src, sib_got, got, first):
-        for lane in range(2):
-            for way in range(2):
-                k = hops[lane][way]
-                if s <= k:
-                    far = k - s + 1
-                    d = zmod(far if way == 0 else -far)
-                    val = src[lane_y[lane], d, core].astype(F32) + sib_got[
-                        lane_y[lane], d
-                    ].astype(F32)
-                    if s > 1:
-                        arrive(first + (lane * 2 + way) * steps + s - 2, got.at[lane, way, s - 2])
-                        val = val + got[lane, way, s - 2].astype(F32)
-                    src[lane_y[lane], d, core] = val.astype(BF16)
-                    send(
-                        first + (lane * 2 + way) * steps + s - 1,
-                        src.at[lane_y[lane], d, core],
-                        got.at[lane, way, s - 1],
-                        znb[way],
-                    )
-
-    def rs_lane(lane, src, sib_got, got, first):
-        val = src[lane_y[lane], z, core].astype(F32) + sib_got[lane_y[lane], z].astype(F32)
-        for way in range(2):
-            k = hops[lane][way]
-            if k:
-                arrive(first + (lane * 2 + way) * steps + k - 1, got.at[lane, way, k - 1])
-                val = val + got[lane, way, k - 1].astype(F32)
-        return val
-
-    def rs_turn(src, sib_got, got, yr, first, y_id):
-        val = rs_lane(1, src, sib_got, got, first)
-        src[1 - y, z, core] = val.astype(BF16)
-        send(y_id, src.at[1 - y, z, core], yr, ynb)
-
-    def rs_end(src, sib_got, got, yr, first, y_id):
-        val = rs_lane(0, src, sib_got, got, first)
-        arrive(y_id, yr)
-        return val + yr[...].astype(F32)
-
-    core_args = (core_b, core_s, core_r)
-    fac_o = (fac_b, fac_s, fac_r)
-    fac_i = (inp_b, inp_s, inp_r)
-
     ag_close()
 
     lat_acc[...] = jnp.zeros_like(lat_acc)
@@ -345,7 +364,8 @@
         return 0
 
     def backward(e, _):
-        pg_acc[...] += dot_nt(outer[e], whole[:, :, :, e].reshape(n_i, n_o))
+        spread = dot_nt(lgrad, whole[:, :, :, e].reshape(n_i, n_o))
+        pg_acc[...] += wide(mix_b[e], n_i) * spread
         return 0
 
     n_om = n_o + 128
@@ -357,20 +377,19 @@
     part_mid[:, :, n_o:n_om] = mix_low.reshape(n_cores, block, 128)
     sum_send(ids.sum_mid, part_mid, got_mid, lat_mix)
 
-    for e in range(n_e):
-        arrive(ids.core_sib + e, core_s.at[:, :, e])
-    rs_step(1, *core_args, ids.core_z)
 
     lax.fori_loop(0, n_e, backward, 0)
     part_mid[:, :, pg_cols] = pg_acc[...].astype(BF16).reshape(n_cores, block, n_i)
     sum_send(ids.sum_mid + n_peers, part_mid, got_mid, pg_cols)
 
+    gate_low = held_a[:, :, :n_g].reshape(rows, n_g)
     expert_full = dot_tn(gate_low, mix_low) * inv_rows
     pick = (
         lax.broadcasted_iota(jnp.int32, (128, 128), 0)
         == lax.broadcasted_iota(jnp.int32, (128, 128), 1) + c * n_e
     ).astype(BF16)
     expert_term = dot_nn(expert_full.astype(BF16), pick)
+    core_step(2)
 
     for k in range(n_peers):
         arrive(ids.factor + k, ef_all.at[behind[k]])
@@ -385,7 +404,7 @@
     held_mid[c, :, n_o:n_og] = (gate_grad * gate * (1.0 - gate)).astype(BF16)
     share_send(ids.share_mid, held_mid, lat_logit)
 
-    rs_step(2, *core_args, ids.core_z)
+    core_step(3)
 
     held_mid[c, :, pg_held] = sum_wait(
         ids.sum_mid + n_peers, part_mid, got_mid, pg_cols
@@ -397,74 +416,71 @@
     logit_grad = held_mid[:, :, n_o:n_og].reshape(rows, n_g)
     blk = (2, n_z, 2)
     g_rows = n_g // n_dp
-    fac_b[:, :, :, :i_rows] = (
+    mid = width // 2
+    w_router = width + mid
+    fac_b[:, :, :, :, :width] = (
         (dot_tn(latent, og[...]) * inv_rows).astype(BF16).reshape(*blk, i_rows, width)
     )
     router_term = (dot_tn(logit_grad, tok[...]) * inv_rows).reshape(*blk, g_rows, width)
-    expert_wide = jnp.concatenate(
-        [expert_term, jnp.zeros((n_g, width - 128), F32)], axis=1
-    ) if width > 128 else expert_term
-    fac_b[:, :, :, i_rows:] = jnp.concatenate(
-        [router_term, expert_wide.reshape(*blk, g_rows, width)], axis=3
+    fac_b[:, :, :, :, width:w_router] = jnp.concatenate(
+        [router_term[..., :mid], router_term[..., mid:]], axis=3
+    ).astype(BF16)
+    expert_blocks = expert_term.reshape(*blk, g_rows, 128)
+    fac_b[:, :, :, :, w_router:] = jnp.concatenate(
+        [expert_blocks, jnp.zeros_like(expert_blocks)], axis=3
     ).astype(BF16)
     send(ids.out_sib, fac_b.at[:, :, 1 - core], fac_s, sib)
 
-    rs_step(3, *core_args, ids.core_z)
+    for s in range(4, steps + 1):
+        core_step(s)
 
     arrive(ids.out_sib, fac_s)
-    rs_step(1, *fac_o, ids.out_z)
+    out_step(1)
 
     share_wait(ids.share_mid + n_peers, held_mid, pg_held)
     pgrad = held_mid[:, :, pg_held].reshape(rows, n_i)
     inp_b[...] = (dot_tn(pgrad, tok[...]) * inv_rows).astype(BF16).reshape(*blk, i_rows, width)
     send(ids.inp_sib, inp_b.at[:, :, 1 - core], inp_s, sib)
 
-    for s in range(4, steps + 1):
-        rs_step(s, *core_args, ids.core_z)
+    out_step(2)
     arrive(ids.inp_sib, inp_s)
-    rs_step(1, *fac_i, ids.inp_z)
-    rs_step(2, *fac_o, ids.out_z)
+    inp_step(1)
 
     mixed_v[...] = dot_nn(latent, outf[...]).astype(BF16)
-    results = [pltpu.make_async_copy(mixed_v, mixed_ref, out_sem.at[0])]
-    results[0].start()
-
-    rs_turn(*core_args, core_yr, ids.core_z, ids.core_y)
-    rs_step(2, *fac_i, ids.inp_z)
-    rs_step(3, *fac_o, ids.out_z)
-    tgrad_v[...] = (dot_nn(pgrad, inf[...]) + dot_nn(logit_grad, rw[...])).astype(BF16)
+    results = []
 
     def result(src, dst):
         results.append(pltpu.make_async_copy(src, dst, out_sem.at[len(results)]))
         results[-1].start()
 
+    result(mixed_v, mixed_ref)
+    core_turn()
+    out_step(3)
+    inp_step(2)
+    tgrad_v[...] = (dot_nn(pgrad, inf[...]) + dot_nn(logit_grad, rw[...])).astype(BF16)
     result(tgrad_v, tgrad_ref)
-    rs_step(3, *fac_i, ids.inp_z)
     for s in range(4, steps + 1):
-        rs_step(s, *fac_o, ids.out_z)
-        rs_step(s, *fac_i, ids.inp_z)
-    rs_turn(*fac_o, fac_yr, ids.out_z, ids.out_y)
-    rs_turn(*fac_i, inp_yr, ids.inp_z, ids.inp_y)
-    cgrad_v[...] = jnp.swapaxes(rs_end(*core_args, core_yr, ids.core_z, ids.core_y), 0, 1)
+        out_step(s)
+        inp_step(s - 1)
+    out_turn()
+    if steps >= 4:
+        inp_step(steps)
+    cgrad_v[...] = jnp.swapaxes(core_end(), 0, 1)
     result(cgrad_v, cgrad_ref)
-    val = rs_end(*fac_o, fac_yr, ids.out_z, ids.out_y)
-    ograd_v[...] = val[:i_rows]
-    rgrad_v[...] = val[i_rows : i_rows + g_rows]
-    egrad_v[...] = val[i_rows + g_rows :, :n_e]
+    inp_turn()
+    val = out_end()
+    ograd_v[...] = val[:, :width]
+    rgrad_v[:, :mid] = val[:g_rows, width:w_router]
+    rgrad_v[:, mid:] = val[g_rows:, width:w_router]
+    egrad_v[...] = val[:g_rows, w_router : w_router + n_e]
     result(ograd_v, ograd_ref)
     result(rgrad_v, rgrad_ref)
     result(egrad_v, egrad_ref)
-    igrad_v[...] = rs_end(*fac_i, inp_yr, ids.inp_z, ids.inp_y)
+    igrad_v[...] = inp_end()
     result(igrad_v, igrad_ref)
 
     for d in sent:
         d.wait_send()
-
-    def drain(e, _):
-        core_sib(e).wait_send()
-        return 0
-
-    lax.fori_loop(0, n_e, drain, 0)
     for r in results:
         r.wait()
 
@@ -504,7 +520,7 @@
     g_rows = n_g // n_dp
     block = rows // n_cores
     cblk = (n_e, i_rows, n_o)
-    fblk = (i_rows + 2 * g_rows, width)
+    fblk = (i_rows, width + width // 2 + 128)
     iblk = (i_rows, width)
     in_cols = n_g + n_i + n_o
     mid_cols = n_o + n_i + 128
@@ -530,19 +546,24 @@
         vmem((i_rows, n_e, n_o), BF16),
         vmem((2, n_z, 2) + cblk, BF16),
         vmem((n_cores, n_e, n_g), F32),
-        vmem((n_cores, block, in_cols), F32),
-        vmem((n_cores - 1, block, in_cols), F32),
-        vmem((n_cores, block, in_cols), BF16),
+        vmem((n_cores, block, n_g + n_o), BF16),
+        vmem((n_cores - 1, block, n_g + n_o), BF16),
+        vmem((n_cores, block, n_g + n_o), BF16),
+        vmem((n_cores, block, n_i), F32),
+        vmem((n_cores - 1, block, n_i), F32),
+        vmem((n_cores, block, n_i), BF16),
         vmem((block, n_g), F32),
         vmem((n_cores, block, mid_cols), BF16),
         vmem((n_cores - 1, block, mid_cols), BF16),
         vmem((n_cores, block, in_cols), BF16),
         vmem((n_e, rows, 128), F32),
-        vmem((n_e, rows, n_o), BF16),
+        vmem((n_cores, block, n_g + n_o), BF16),
+        vmem((n_e, rows, 128), F32),
+        vmem((2 * n_z, 2, i_rows, rows), BF16),
+        vmem((2 * n_z, i_rows, rows), BF16),
         vmem((rows, n_o), F32),
         vmem((rows, n_i), F32),
         vmem((rows, 128), F32),
-        vmem((2, n_z, 2) + cblk, BF16),
         vmem((2, n_z) + cblk, BF16),
         vmem((2, 2, steps) + cblk, BF16),
         vmem(cblk, BF16),

time: 93.4 us -> 89.2 us (0.955)
  Pallas kernels: 92.1 us -> 88.4 us
    pallas_call x1, Pallas kernels: 90 us -> 86.3 us  [shards(): pl.pallas_call(functools.partial(kernel, n_z, n_cores), out_shape=results...]
where the time goes in v4:
time: 89.2 us; the launch traced here: 89 us
  Pallas kernels  88.4 us (99%)
    pallas_call x1, Pallas kernels, shards(): pl.pallas_call(functools.partial(kernel, n_z, n_cores), out_shape=results...  86.3 us
    pallas_call x1, Pallas kernels, shards(): pl.pallas_call(functools.partial(hand_over, len(results)), out_shape=resu...  2.11 us

profile of v4, /device:TPU:2, one launch (start us, length us, event | category | flops | bytes accessed | tf_op | source)
XLA Modules:
  0.0 89.0 jit_solution(13234976395494926978)
XLA Ops:
  0.6 86.3 %shard_map.126 = (bf16[256,768]{1,0:T(8,128)(2,1)}, bf16[256,768]{1,0:T(8,128)(2,1)}, f32[16,8,512]{2,1,0:T(8,128)}, f32[16,768]{1,0:T(8,128)}, f32[8,768]{1,0:T...) custom-call(bf16[256,768]{1,0:T(8,128)(2,1)} %tok_hbm.1, bf16[256,768]{1,0:T(8,128)(2,1)} %rw_hbm.1, bf16[8,256]{1,0:T(8,128)(2,1)} %bitcast.1, ...), custom_call_target="tpu_custom_call" | custom-call | tf_op jit(solution)/shard_map/pallas_call | solution.py:583
  86.9 2.1 %shard_map.127 = (bf16[256,768]{1,0:T(8,128)(2,1)}, bf16[256,768]{1,0:T(8,128)(2,1)}, f32[16,8,512]{2,1,0:T(8,128)}, f32[16,768]{1,0:T(8,128)}, f32[8,768]{1,0:T...) custom-call(bf16[256,768]{1,0:T(8,128)(2,1)} %get-tuple-element.14.refs_0_, bf16[256,768]{1,0:T(8,128)(2,1)} %get-tuple-element.15.refs_1_, ...), custom_call_target="tpu_custom_call" | custom-call | tf_op jit(solution)/shard_map/pallas_call | solution.py:593

commit v5 on v4

--- a/solution.py
+++ b/solution.py
@@ -245,6 +245,7 @@
 
     ag_step(2, 1)
     ag_step(3, 0)
+    ag_step(3, 1)
 
     def wide(v, n):
         return jnp.concatenate([v] * (n // 128), axis=1)
@@ -259,8 +260,6 @@
     spread_mixing(held_a, mix_b)
     lgrad = held_a[:, :, n_g:].reshape(rows, n_o)
     lgrad_wide = lgrad.astype(F32)
-
-    ag_step(3, 1)
 
     share_wait(ids.share_in + n_peers, held_p, everything)
     proj = held_p[...].reshape(rows, n_i)
@@ -410,6 +409,8 @@
         ids.sum_mid + n_peers, part_mid, got_mid, pg_cols
     ).astype(BF16)
     share_send(ids.share_mid + n_peers, held_mid, pg_held)
+    for s in range(4, steps + 1):
+        core_step(s)
 
     share_wait(ids.share_mid, held_mid, lat_logit)
     latent = held_mid[:, :, :n_o].reshape(rows, n_o)
@@ -431,8 +432,6 @@
     ).astype(BF16)
     send(ids.out_sib, fac_b.at[:, :, 1 - core], fac_s, sib)
 
-    for s in range(4, steps + 1):
-        core_step(s)
 
     arrive(ids.out_sib, fac_s)
     out_step(1)

time: 89.2 us -> 88.8 us (level)
  no operation moved by 1% of the time
where the time goes in v5:
time: 88.8 us; the launch traced here: 88.7 us
  Pallas kernels  88 us (99%)
    pallas_call x1, Pallas kernels, shards(): pl.pallas_call(functools.partial(kernel, n_z, n_cores), out_shape=results...  85.9 us
    pallas_call x1, Pallas kernels, shards(): pl.pallas_call(functools.partial(hand_over, len(results)), out_shape=resu...  2.11 us

profile of v5, /device:TPU:2, one launch (start us, length us, event | category | flops | bytes accessed | tf_op | source)
XLA Modules:
  0.0 88.7 jit_solution(11231362507580749319)
XLA Ops:
  0.6 85.9 %shard_map.126 = (bf16[256,768]{1,0:T(8,128)(2,1)}, bf16[256,768]{1,0:T(8,128)(2,1)}, f32[16,8,512]{2,1,0:T(8,128)}, f32[16,768]{1,0:T(8,128)}, f32[8,768]{1,0:T...) custom-call(bf16[256,768]{1,0:T(8,128)(2,1)} %tok_hbm.1, bf16[256,768]{1,0:T(8,128)(2,1)} %rw_hbm.1, bf16[8,256]{1,0:T(8,128)(2,1)} %bitcast.1, ...), custom_call_target="tpu_custom_call" | custom-call | tf_op jit(solution)/shard_map/pallas_call | solution.py:582
  86.6 2.1 %shard_map.127 = (bf16[256,768]{1,0:T(8,128)(2,1)}, bf16[256,768]{1,0:T(8,128)(2,1)}, f32[16,8,512]{2,1,0:T(8,128)}, f32[16,768]{1,0:T(8,128)}, f32[8,768]{1,0:T...) custom-call(bf16[256,768]{1,0:T(8,128)(2,1)} %get-tuple-element.14.refs_0_, bf16[256,768]{1,0:T(8,128)(2,1)} %get-tuple-element.15.refs_1_, ...), custom_call_target="tpu_custom_call" | custom-call | tf_op jit(solution)/shard_map/pallas_call | solution.py:592

commit v6 on v5

--- a/solution.py
+++ b/solution.py
@@ -433,6 +433,14 @@
     send(ids.out_sib, fac_b.at[:, :, 1 - core], fac_s, sib)
 
 
+    mixed_v[...] = dot_nn(latent, outf[...]).astype(BF16)
+    results = []
+
+    def result(src, dst):
+        results.append(pltpu.make_async_copy(src, dst, out_sem.at[len(results)]))
+        results[-1].start()
+
+    result(mixed_v, mixed_ref)
     arrive(ids.out_sib, fac_s)
     out_step(1)
 
@@ -442,22 +450,14 @@
     send(ids.inp_sib, inp_b.at[:, :, 1 - core], inp_s, sib)
 
     out_step(2)
+    tgrad_v[...] = (dot_nn(pgrad, inf[...]) + dot_nn(logit_grad, rw[...])).astype(BF16)
+    result(tgrad_v, tgrad_ref)
     arrive(ids.inp_sib, inp_s)
     inp_step(1)
 
-    mixed_v[...] = dot_nn(latent, outf[...]).astype(BF16)
-    results = []
-
-    def result(src, dst):
-        results.append(pltpu.make_async_copy(src, dst, out_sem.at[len(results)]))
-        results[-1].start()
-
-    result(mixed_v, mixed_ref)
     core_turn()
     out_step(3)
     inp_step(2)
-    tgrad_v[...] = (dot_nn(pgrad, inf[...]) + dot_nn(logit_grad, rw[...])).astype(BF16)
-    result(tgrad_v, tgrad_ref)
     for s in range(4, steps + 1):
         out_step(s)
         inp_step(s - 1)

time: 88.8 us -> 88.8 us (level)
  no operation moved by 1% of the time
where the time goes in v6:
time: 88.8 us; the launch traced here: 88.7 us
  Pallas kernels  88 us (99%)
    pallas_call x1, Pallas kernels, shards(): pl.pallas_call(functools.partial(kernel, n_z, n_cores), out_shape=results...  85.9 us
    pallas_call x1, Pallas kernels, shards(): pl.pallas_call(functools.partial(hand_over, len(results)), out_shape=resu...  2.11 us

profile of v6, /device:TPU:2, one launch (start us, length us, event | category | flops | bytes accessed | tf_op | source)
XLA Modules:
  0.0 88.7 jit_solution(8438254491809322134)
XLA Ops:
  0.6 85.9 %shard_map.126 = (bf16[256,768]{1,0:T(8,128)(2,1)}, bf16[256,768]{1,0:T(8,128)(2,1)}, f32[16,8,512]{2,1,0:T(8,128)}, f32[16,768]{1,0:T(8,128)}, f32[8,768]{1,0:T...) custom-call(bf16[256,768]{1,0:T(8,128)(2,1)} %tok_hbm.1, bf16[256,768]{1,0:T(8,128)(2,1)} %rw_hbm.1, bf16[8,256]{1,0:T(8,128)(2,1)} %bitcast.1, ...), custom_call_target="tpu_custom_call" | custom-call | tf_op jit(solution)/shard_map/pallas_call | solution.py:582
  86.6 2.1 %shard_map.127 = (bf16[256,768]{1,0:T(8,128)(2,1)}, bf16[256,768]{1,0:T(8,128)(2,1)}, f32[16,8,512]{2,1,0:T(8,128)}, f32[16,768]{1,0:T(8,128)}, f32[8,768]{1,0:T...) custom-call(bf16[256,768]{1,0:T(8,128)(2,1)} %get-tuple-element.14.refs_0_, bf16[256,768]{1,0:T(8,128)(2,1)} %get-tuple-element.15.refs_1_, ...), custom_call_target="tpu_custom_call" | custom-call | tf_op jit(solution)/shard_map/pallas_call | solution.py:592
